TPU v7x, 512 devices: a whole 4x4x16 slice. The times are simulated.
512 devices in a mesh: tm: 32 (over z, core), space: 16 (over y, x).
Axes of the slice: x: 4, y: 4, z: 16, core: 2. Of those that a mesh axis runs over, the one named last changes fastest.
Arguments:
- blocks: bfloat16 [1536, 48, 48, 128], P(('tm', 'space')), may hold values from -12 to 12
- fields: float32 [1536, 48, 144], P(('tm', 'space')), may hold values from -4 to 4
- trial: bfloat16 [48, 48, 48, 128], P('space'), may hold values from -6 to 6
Outputs:
- handed: bfloat16 [1536, 48, 48, 128], P(('tm', 'space'))
- projection: float32 [1024, 32], P('tm')
All inputs are finite; a program needn't handle non-finite values.
Results may differ from a plain program's by a relative error of at most 0.006.
Values may be sent and summed in bfloat16 or wider, within the bound.
A program may use at most 64 MiB of HBM per device.

v0:
```python
import math

import jax
import jax.numpy as jnp
from jax import lax
from jax.sharding import PartitionSpec as P

L = 48
C4 = 4
ORB = 32


KINETIC = 0.0716
MIX_SCALAR = 0.25
MIX_ISOSPIN = 0.15


def from_behind(value, axis, steps):
    count = lax.axis_size(axis)
    pairs = [(source, (source + steps) % count) for source in range(count)]
    return lax.ppermute(value, axis, pairs)


def kinetic_table(length):
    indices = jnp.arange(length, dtype=jnp.int32) - length // 2
    positions = jnp.arange(length, dtype=jnp.int32)
    offset = positions[:, None] - positions[None, :]
    phases = indices[:, None, None] * offset[None, :, :] % length
    momenta = 2.0 * math.pi / length * indices.astype(jnp.float32)
    damping = jnp.exp(-0.5 * KINETIC * momenta * momenta)
    angles = 2.0 * math.pi / length * phases.astype(jnp.float32)
    return jnp.sum(damping[:, None, None] * jnp.cos(angles), axis=0) / length


def along_first(kernel, wavefn):
    return jnp.einsum("ux,xabk->uabk", kernel, wavefn, precision=lax.Precision.HIGHEST)


def along_second(kernel, wavefn):
    return jnp.einsum("uy,ayzk->auzk", kernel, wavefn, precision=lax.Precision.HIGHEST)


def along_third(kernel, wavefn):
    return jnp.einsum("uz,ayzk->ayuk", kernel, wavefn, precision=lax.Precision.HIGHEST)


def mixing(wavefn, auxiliary):
    length = wavefn.shape[2]
    scalar = auxiliary[..., :length][..., None]
    flavour = auxiliary[..., length : 2 * length][..., None]
    charge = auxiliary[..., 2 * length :][..., None]
    midpoint = wavefn.shape[3] // 2
    lower_iso = wavefn[..., :midpoint]
    upper_iso = wavefn[..., midpoint:]
    diagonal_term = 1.0 + MIX_SCALAR * scalar
    new_lower = (
        diagonal_term + MIX_ISOSPIN * charge
    ) * lower_iso + MIX_ISOSPIN * flavour * upper_iso
    new_upper = (
        diagonal_term - MIX_ISOSPIN * charge
    ) * upper_iso + MIX_ISOSPIN * flavour * lower_iso
    return jnp.concatenate([new_lower, new_upper], axis=3)


def measure(trial, current):
    sites_dev = trial.shape[0] * trial.shape[1] * trial.shape[2]
    partial_value = jnp.einsum(
        "nco,ncp->op",
        trial.reshape(sites_dev, C4, ORB).astype(jnp.float32),
        current.reshape(sites_dev, C4, ORB),
        precision=lax.Precision.HIGHEST,
    )
    summed = lax.psum(partial_value, "space")
    return summed / math.sqrt(C4 * L**3)


def body(blocks, fields, trial):
    kernel = kinetic_table(blocks.shape[1])
    current = blocks.astype(jnp.float32)
    current = along_second(kernel, along_third(kernel, current))
    current = along_first(
        kernel, lax.all_to_all(current, "space", split_axis=1, concat_axis=0, tiled=True)
    )
    own_pencil = lax.all_to_all(
        fields.astype(jnp.bfloat16), "space", split_axis=1, concat_axis=0, tiled=True
    ).astype(fields.dtype)
    current = mixing(current, own_pencil)
    current = from_behind(current, "tm", 1)
    current = along_third(kernel, along_first(kernel, current))
    current = along_second(
        kernel, lax.all_to_all(current, "space", split_axis=0, concat_axis=1, tiled=True)
    )
    current = mixing(current, fields)
    measured = measure(trial, current)
    rounded = current.astype(jnp.bfloat16)
    measured = from_behind(measured, "tm", -1)
    handed = from_behind(rounded, "tm", 1)
    return (handed, measured)


def solution(mesh):
    in_specs = (
        P(("tm", "space"), None, None, None),
        P(("tm", "space"), None, None),
        P("space", None, None, None),
    )
    out_specs = (P(("tm", "space"), None, None, None), P("tm", None))
    return jax.shard_map(body, mesh=mesh, in_specs=in_specs, out_specs=out_specs, check_vma=False)
```

profile of v0, /device:TPU:1, one launch (start us, length us, event | category | flops | bytes accessed | tf_op | source)
XLA Modules:
  0.0 328.3 jit_solution(12224359001787628156)
XLA Ops:
  0.6 0.0 copy-start
  0.6 1.1 convert_element_type.32
  1.7 0.1 copy.111
  1.8 0.8 reshape.61
  2.5 7.6 %all-to-all-start = ((bf16[16,2,648]{2,1,0:T(2,128)(2,1)}), bf16[16,2,648]{2,1,0:T(2,128)(2,1)S(1)}, u32[]{:S(2)}, u32[]{:S(2)}) async-start(bf16[16,2,648]{2,1,0:T(2,128)(2,1)} %reshape.61), calls=%async_computation | async-start | bytes 98304 | tf_op jit(solution)/shard_map/all_to_all | solution.py:84
  10.2 5.1 %fusion.21 = f32[48,48]{1,0:T(8,128)S(1)} fusion(s32[48,48]{1,0:T(8,128)S(1)} %iota_subtract_fusion, s32[48]{0:T(128)S(1)} %iota_add_fusion, f32[48]{0:T(128)S(1)} %multiply_exponential_fusion), kind=kLoop, calls=%fused_computation.23 | loop fusion | flops 1214208 | bytes 18816 | tf_op jit(solution)/shard_map/reduce_sum | solution.py:32
  15.3 1.6 convolution_bitcast_fusion
  16.8 4.6 %fusion.8 = f32[3,48,48,128]{3,1,2,0:T(8,128)S(1)} fusion(f32[3,48,48,128]{3,2,1,0:T(8,128)S(1)} %convolution_bitcast_fusion, f32[48,48]{1,0:T(8,128)S(1)} %fusion.21), kind=kOutput, calls=%fused_computation.14 | convolution fusion | flops 509610240 | bytes 7087104 | tf_op jit(solution)/shard_map/uy,ayzk->auzk/dot_general | solution.py:40
  21.4 2.9 copy.78
  24.3 6.7 %all-to-all-start.1 = ((f32[3,48,48,128]{3,2,0,1:T(8,128)}), f32[3,48,48,128]{3,2,0,1:T(8,128)}, u32[]{:S(2)}, u32[]{:S(2)}) async-start(f32[3,48,48,128]{3,2,0,1:T(8,128)} %copy.78), calls=%async_computation.1 | async-start | bytes 7077888 | tf_op jit(solution)/shard_map/all_to_all | solution.py:82
  31.0 0.2 reshape.62
  31.2 0.1 reshape.58
  31.2 0.1 copy.75
  31.3 0.1 reshape.57
  31.4 0.1 fusion.29
  31.5 0.1 copy.82
  31.6 0.1 copy.76
  31.7 0.1 copy.83
  31.8 44.2 %all-to-all-done.1 = f32[3,48,48,128]{3,2,0,1:T(8,128)} async-done(((f32[3,48,48,128]{3,2,0,1:T(8,128)}), f32[3,48,48,128]{3,2,0,1:T(8,128)}, u32[]{:S(2)}, u32[]{:S(2)}) %all-to-all-start.1) | async-done | bytes 3538976 | tf_op jit(solution)/shard_map/all_to_all | solution.py:82
  76.0 2.2 copy.80
  78.3 4.2 %fusion.4 = f32[48,3,48,128]{3,0,2,1:T(8,128)S(1)} fusion(f32[48,3,48,128]{3,2,1,0:T(8,128)S(1)} %bitcast.55, f32[48,48]{1,0:T(8,128)S(1)} %fusion.21), kind=kOutput, calls=%fused_computation.6 | convolution fusion | flops 509610240 | bytes 7087104 | tf_op jit(solution)/shard_map/ux,xabk->uabk/dot_general | solution.py:36
  82.5 4.6 %multiply_add_fusion.3 = (f32[48,3,48,64]{3,0,2,1:T(8,128)S(1)}, f32[48,3,48,64]{3,0,2,1:T(8,128)S(1)}) fusion(f32[48,3,48,128]{3,0,2,1:T(8,128)S(1)} %fusion.4, f32[48,3,48]{0,2,1:T(8,128)S(1)} %copy.82, f32[48,3,48]{0,2,1:T(8,128)S(1)} %copy.76, f32[48,3,48]{0,2,1:T(8,128)S(1)} %copy.83), kind=kLoop, calls=%fused_computation.13 | loop fusion | flops 2654208 | bytes 7160832 | tf_op jit(solution)/shard_map/add | solution.py:56
  87.1 1.0 pad_maximum_fusion
  88.1 9.9 %collective-permute-start = (f32[48,3,48,128]{3,0,2,1:T(8,128)S(1)}, f32[48,3,48,128]{3,0,2,1:T(8,128)S(1)}, u32[]{:S(2)}, u32[]{:S(2)}) collective-permute-start(f32[48,3,48,128]{3,0,2,1:T(8,128)S(1)} %pad_maximum_fusion), channel_id=1, source_target_pairs={{0,16},{16,32},{32,48},{48,64},{64,80},{80,96},{96,112},{112,128},... | collective-permute-start | bytes 10616840 | tf_op jit(solution)/shard_map/ppermute | solution.py:21
  98.0 38.4 %collective-permute-done = f32[48,3,48,128]{3,0,2,1:T(8,128)S(1)} collective-permute-done((f32[48,3,48,128]{3,0,2,1:T(8,128)S(1)}, f32[48,3,48,128]{3,0,2,1:T(8,128)S(1)}, u32[]{:S(2)}, u32[]{:S(2)}) %collective-permute-start) | collective-permute-done | bytes 3538976 | tf_op jit(solution)/shard_map/ppermute | solution.py:21
  136.4 3.3 %fusion.32 = f32[48,3,48,128]{3,0,2,1:T(8,128)S(1)} fusion(f32[48,3,48,128]{3,0,2,1:T(8,128)S(1)} %collective-permute-done, f32[48,48]{1,0:T(8,128)S(1)} %fusion.21), kind=kOutput, calls=%fused_computation.43 | convolution fusion | flops 509610240 | bytes 7087104 | tf_op jit(solution)/shard_map/ux,xabk->uabk/dot_general | solution.py:36
  139.8 6.2 %fusion.11 = f32[48,3,48,128]{3,2,1,0:T(8,128)} fusion(f32[48,3,48,128]{3,0,2,1:T(8,128)S(1)} %fusion.32, f32[48,48]{1,0:T(8,128)S(1)} %fusion.21), kind=kOutput, calls=%fused_computation.15 | convolution fusion | flops 509610240 | bytes 7087104 | tf_op jit(solution)/shard_map/uz,ayzk->ayuk/dot_general | solution.py:44
  146.0 4.9 %all-to-all-start.2 = ((f32[48,3,48,128]{3,2,1,0:T(8,128)}), f32[48,3,48,128]{3,2,1,0:T(8,128)}, u32[]{:S(2)}, u32[]{:S(2)}) async-start(f32[48,3,48,128]{3,2,1,0:T(8,128)} %fusion.11), calls=%async_computation.2 | async-start | bytes 7077888 | tf_op jit(solution)/shard_map/all_to_all | solution.py:91
  150.9 0.1 fusion.27
  151.0 0.1 copy.87
  151.1 0.1 copy.72
  151.2 0.1 copy.88
  151.3 39.1 %all-to-all-done.2 = f32[48,3,48,128]{3,2,1,0:T(8,128)} async-done(((f32[48,3,48,128]{3,2,1,0:T(8,128)}), f32[48,3,48,128]{3,2,1,0:T(8,128)}, u32[]{:S(2)}, u32[]{:S(2)}) %all-to-all-start.2) | async-done | bytes 3538976 | tf_op jit(solution)/shard_map/all_to_all | solution.py:91
  190.4 2.3 copy.85
  192.7 4.6 %fusion.14 = f32[3,48,48,128]{3,1,2,0:T(8,128)S(1)} fusion(f32[3,48,48,128]{3,2,1,0:T(8,128)S(1)} %bitcast.54, f32[48,48]{1,0:T(8,128)S(1)} %fusion.21), kind=kOutput, calls=%fused_computation.16 | convolution fusion | flops 509610240 | bytes 7087104 | tf_op jit(solution)/shard_map/uy,ayzk->auzk/dot_general | solution.py:40
  197.3 4.3 %multiply_add_fusion.1 = (f32[3,48,48,64]{3,1,2,0:T(8,128)S(1)}, f32[3,48,48,64]{3,1,2,0:T(8,128)S(1)}) fusion(f32[3,48,48,128]{3,1,2,0:T(8,128)S(1)} %fusion.14, f32[3,48,48]{1,2,0:T(8,128)S(1)} %copy.87, f32[3,48,48]{1,2,0:T(8,128)S(1)} %copy.72, f32[3,48,48]{1,2,0:T(8,128)S(1)} %copy.88), kind=kLoop, calls=%fused_computation.11 | loop fusion | flops 2654208 | bytes 7160832 | tf_op jit(solution)/shard_map/add | solution.py:56
  201.7 3.4 %fusion.55 = (bf16[3,48,48,128]{3,1,2,0:T(8,128)(2,1)}, f32[3,48,48,128]{3,1,2,0:T(8,128)}) fusion(f32[3,48,48,64]{3,1,2,0:T(8,128)S(1)} %get-tuple-element.15, f32[3,48,48,64]{3,1,2,0:T(8,128)S(1)} %get-tuple-element.14), kind=kLoop, calls=%fused_computation.70 | loop fusion | flops 1769472 | bytes 8847360 | tf_op jit(solution)/shard_map/convert_element_type | solution.py:95
  205.0 15.9 %collective-permute-start.1 = (bf16[3,48,48,128]{3,1,2,0:T(8,128)(2,1)}, bf16[3,48,48,128]{3,1,2,0:T(8,128)(2,1)}, u32[]{:S(2)}, u32[]{:S(2)}) collective-permute-start(bf16[3,48,48,128]{3,1,2,0:T(8,128)(2,1)} %get-tuple-element.12), channel_id=1, source_target_pairs={{0,16},{16,32},{32,48},{48,64},{64,80},{80,96},{96,112},{112,128},... | collective-permute-start | bytes 5308424 | tf_op jit(solution)/shard_map/ppermute | solution.py:21
  221.0 4.3 %copy.90 = bf16[3,48,48,128]{2,1,0,3:T(8,128)(2,1)} copy(bf16[3,48,48,128]{3,2,1,0:T(8,128)(2,1)S(1)} %copy-done.2) | data formatting | bytes 3538944 | tf_op args[2]
  225.3 6.5 %reshape.56 = bf16[6912,4,32]{0,2,1:T(8,128)(2,1)S(1)} reshape(bf16[3,48,48,128]{2,1,0,3:T(8,128)(2,1)} %copy.90) | data formatting | bytes 3538944 | tf_op jit(solution)/shard_map/reshape | solution.py:69
  231.8 7.8 %copy.89 = f32[3,48,48,128]{2,1,0,3:T(8,128)} copy(f32[3,48,48,128]{3,1,2,0:T(8,128)} %get-tuple-element.13) | data formatting | bytes 7077888 | tf_op jit(solution)/shard_map/concatenate | solution.py:62
  239.6 8.4 %reshape.55 = f32[6912,4,32]{0,2,1:T(8,128)} reshape(f32[3,48,48,128]{2,1,0,3:T(8,128)} %copy.89) | data formatting | bytes 7077888 | tf_op jit(solution)/shard_map/reshape | solution.py:70
  247.9 3.7 %convolution_bitcast_fusion.1 = f32[32,32]{0,1:T(8,128)S(1)} fusion(f32[6912,4,32]{0,2,1:T(8,128)} %reshape.55, bf16[6912,4,32]{0,2,1:T(8,128)(2,1)S(1)} %reshape.56), kind=kOutput, calls=%fused_computation.28 | convolution fusion | flops 339738624 | bytes 5312512 | tf_op jit(solution)/shard_map/nco,ncp->op/dot_general | solution.py:67
  251.6 57.2 %psum.7 = f32[32,32]{0,1:T(8,128)S(1)} all-reduce(f32[32,32]{0,1:T(8,128)S(1)} %convolution_bitcast_fusion.1), channel_id=1, replica_groups=mesh['tm'=32,'space'=16] {'space'}, use_global_device_ids=true, to_apply=%region_1.2 | all-reduce | flops 1024 | bytes 8192 | tf_op jit(solution)/shard_map/psum | solution.py:73
  308.8 5.3 %collective-permute-start.2 = (f32[32,32]{0,1:T(8,128)S(1)}, f32[32,32]{0,1:T(8,128)S(1)}, u32[]{:S(2)}, u32[]{:S(2)}) collective-permute-start(f32[32,32]{0,1:T(8,128)S(1)} %broadcast_multiply_fusion), channel_id=1, source_target_pairs={{0,496},{16,0},{32,16},{48,32},{64,48},{80,64},{96,80},{112,96},{1... | collective-permute-start | bytes 12296 | tf_op jit(solution)/shard_map/ppermute | solution.py:21
  314.1 10.3 %collective-permute-done.2 = f32[32,32]{0,1:T(8,128)S(1)} collective-permute-done((f32[32,32]{0,1:T(8,128)S(1)}, f32[32,32]{0,1:T(8,128)S(1)}, u32[]{:S(2)}, u32[]{:S(2)}) %collective-permute-start.2) | collective-permute-done | bytes 4128 | tf_op jit(solution)/shard_map/ppermute | solution.py:21
  324.5 0.7 copy.92
  325.1 3.1 copy.91
  (14 shorter events, 0.1 us)
Async XLA Ops:
  0.6 14.6 %copy-start = (bf16[3,48,48,128]{3,2,1,0:T(8,128)(2,1)S(1)}, bf16[3,48,48,128]{3,2,1,0:T(8,128)(2,1)}, u32[]{:S(2)}) copy-start(bf16[3,48,48,128]{3,2,1,0:T(8,128)(2,1)} %param.3) | copy-start | bytes 5308420
  2.5 21.7 %all-to-all-start = ((bf16[16,2,648]{2,1,0:T(2,128)(2,1)}), bf16[16,2,648]{2,1,0:T(2,128)(2,1)S(1)}, u32[]{:S(2)}, u32[]{:S(2)}) async-start(bf16[16,2,648]{2,1,0:T(2,128)(2,1)} %reshape.61), calls=%async_computation | async-start | bytes 98304 | tf_op jit(solution)/shard_map/all_to_all | solution.py:84
  24.3 51.7 %all-to-all-start.1 = ((f32[3,48,48,128]{3,2,0,1:T(8,128)}), f32[3,48,48,128]{3,2,0,1:T(8,128)}, u32[]{:S(2)}, u32[]{:S(2)}) async-start(f32[3,48,48,128]{3,2,0,1:T(8,128)} %copy.78), calls=%async_computation.1 | async-start | bytes 7077888 | tf_op jit(solution)/shard_map/all_to_all | solution.py:82
  88.1 48.3 %collective-permute-start = (f32[48,3,48,128]{3,0,2,1:T(8,128)S(1)}, f32[48,3,48,128]{3,0,2,1:T(8,128)S(1)}, u32[]{:S(2)}, u32[]{:S(2)}) collective-permute-start(f32[48,3,48,128]{3,0,2,1:T(8,128)S(1)} %pad_maximum_fusion), channel_id=1, source_target_pairs={{0,16},{16,32},{32,48},{48,64},{64,80},{80,96},{96,112},{112,128},... | collective-permute-start | bytes 10616840 | tf_op jit(solution)/shard_map/ppermute | solution.py:21
  146.0 4.9 %copy-start.3 = (f32[3,48,144]{2,1,0:T(8,128)S(1)}, f32[3,48,144]{2,1,0:T(8,128)}, u32[]{:S(2)}) copy-start(f32[3,48,144]{2,1,0:T(8,128)} %param.4) | copy-start | bytes 248836
  146.0 44.4 %all-to-all-start.2 = ((f32[48,3,48,128]{3,2,1,0:T(8,128)}), f32[48,3,48,128]{3,2,1,0:T(8,128)}, u32[]{:S(2)}, u32[]{:S(2)}) async-start(f32[48,3,48,128]{3,2,1,0:T(8,128)} %fusion.11), calls=%async_computation.2 | async-start | bytes 7077888 | tf_op jit(solution)/shard_map/all_to_all | solution.py:91
  201.7 19.3 %copy-start.2 = (bf16[3,48,48,128]{3,2,1,0:T(8,128)(2,1)S(1)}, bf16[3,48,48,128]{3,2,1,0:T(8,128)(2,1)}, u32[]{:S(2)}) copy-start(bf16[3,48,48,128]{3,2,1,0:T(8,128)(2,1)} %param.5) | copy-start | bytes 5308420
  205.0 120.1 %collective-permute-start.1 = (bf16[3,48,48,128]{3,1,2,0:T(8,128)(2,1)}, bf16[3,48,48,128]{3,1,2,0:T(8,128)(2,1)}, u32[]{:S(2)}, u32[]{:S(2)}) collective-permute-start(bf16[3,48,48,128]{3,1,2,0:T(8,128)(2,1)} %get-tuple-element.12), channel_id=1, source_target_pairs={{0,16},{16,32},{32,48},{48,64},{64,80},{80,96},{96,112},{112,128},... | collective-permute-start | bytes 5308424 | tf_op jit(solution)/shard_map/ppermute | solution.py:21
  239.6 88.7 %copy-start.1 = (bf16[3,48,48,128]{3,2,1,0:T(8,128)(2,1)S(1)}, bf16[3,48,48,128]{3,2,1,0:T(8,128)(2,1)}, u32[]{:S(2)}) copy-start(bf16[3,48,48,128]{3,2,1,0:T(8,128)(2,1)} %param.3) | copy-start | bytes 5308420
  308.8 15.6 %collective-permute-start.2 = (f32[32,32]{0,1:T(8,128)S(1)}, f32[32,32]{0,1:T(8,128)S(1)}, u32[]{:S(2)}, u32[]{:S(2)}) collective-permute-start(f32[32,32]{0,1:T(8,128)S(1)} %broadcast_multiply_fusion), channel_id=1, source_target_pairs={{0,496},{16,0},{32,16},{48,32},{64,48},{80,64},{96,80},{112,96},{1... | collective-permute-start | bytes 12296 | tf_op jit(solution)/shard_map/ppermute | solution.py:21
where the time goes:
time: 331 us; the launch traced here: 328 us
  waiting for transfers between devices  132 us (40%)
  blocking collectives  57.2 us (17%)
  starting transfers between devices  50.4 us (15%)
  local copies, waits for them, and re-layouts  40 us (12%)
  matrix products  28.2 us (9%)
  other arithmetic  19.6 us (6%)
    psum x1, blocking collectives, measure(): summed = lax.psum(partial_value, 'space')  57.2 us
    ppermute x3, waiting for transfers between devices, from_behind(): return lax.ppermute(value, axis, pairs)  48.8 us
    all_to_all x1, waiting for transfers between devices, body(): lax.all_to_all(current, 'space', split_axis=1, concat_axis=0, tiled=True)  44.2 us
    all_to_all x1, waiting for transfers between devices, body(): lax.all_to_all(current, 'space', split_axis=0, concat_axis=1, tiled=True)  39.1 us
    ppermute x3, starting transfers between devices, from_behind(): return lax.ppermute(value, axis, pairs)  31.1 us
    dot_general x2, matrix products, along_second(): jnp.einsum('uy,ayzk->auzk', kernel, wavefn, precision=lax.Precision.HIGHEST)  9.12 us
    unnamed x13, local copies, waits for them, and re-layouts  9.09 us
    add x2, other arithmetic, mixing(): (diagonal_term + MIX_ISOSPIN * charge) * lower_iso  8.9 us
  transfers between devices with their start and end apart: 6, of which 4 were waited for; matrix products, arithmetic and copies ran while one was open for 14% of the time, Pallas kernels for 0%

commit v1 on v0

v1 whole, which is shorter than its diff:
```python
import math

import jax
import jax.numpy as jnp
import ml_dtypes
import numpy as np
from jax import lax
from jax.experimental import pallas as pl
from jax.experimental.pallas import tpu as pltpu
from jax.sharding import PartitionSpec as P

L = 48
C4 = 4
ORB = 32
K = C4 * ORB

KINETIC = 0.0716
MIX_SCALAR = 0.25
MIX_ISOSPIN = 0.15

TM = 32
GRID = 4
SPACE = GRID * GRID
R = L // SPACE
ZS = 16
G = L // ZS
ROWS = L * ZS
TRI = G * R * ZS
MESH = pl.DeviceIdType.MESH


def tables():
    modes = np.arange(L) - L // 2
    damping = np.exp(-0.5 * KINETIC * (2 * math.pi / L * modes) ** 2)
    sites = np.arange(L)
    offset = sites[:, None] - sites[None, :]
    kernel = (damping[:, None, None] * np.cos(2 * math.pi / L * modes[:, None, None] * offset)).sum(0) / L
    diagonal = float(kernel[0, 0])
    unit = kernel / diagonal

    major = np.kron(unit, np.eye(ZS))
    minor = np.einsum("azbw,xy->axzbyw", unit.reshape(G, ZS, G, ZS), np.eye(R)).reshape(TRI, TRI)

    lanes = np.zeros((3 * L, 3 * K))
    for z in range(L):
        lanes[z, z] = 1
        lanes[2 * L + z, L + z] = 1
        lanes[L + z, K + z] = 1
        lanes[L + z, 2 * K + L + z] = 1
    pack = np.zeros((SPACE, 16, 3, R, L))
    for j in range(SPACE):
        for x in range(R):
            for y in range(R):
                n = x * R + y
                pack[j, n, 0, x, R * j + y] = 1
                pack[j, 9 + n // 2, 1 + n % 2, x, R * j + y] = 1
    pack = pack.reshape(SPACE * 16, 3 * R * L)
    pick = np.zeros((2, R, G, R, ZS, 16))
    keep = np.zeros((2, R, G, R, ZS, K))
    for y in range(R):
        for x in range(R):
            n = x * R + y
            pick[0, y, :, x, :, n] = 1
            pick[1, y, :, x, :, 9 + n // 2] = 1
            for g in range(G):
                for z in range(ZS):
                    keep[0, y, g, x, z, [ZS * g + z, L + ZS * g + z]] = 1
                    keep[1, y, g, x, z, L * (n % 2) + ZS * g + z] = 1
    pick = pick.reshape(2 * R * TRI, 16)
    keep = keep.reshape(2 * R * TRI, K)
    spread = np.kron(np.eye(L), np.ones((ZS, 1)))
    keep_z = np.zeros((G, ZS, 2 * K))
    for g in range(G):
        for z in range(ZS):
            keep_z[g, z, [ZS * g + z, L + ZS * g + z, K + ZS * g + z]] = 1
    fill = np.zeros((2 * K, 2 * K))
    fill[:L, :K] = 1
    fill[L : 2 * L, : K // 2] = 1
    fill[L : 2 * L, K // 2 : K] = -1
    fill[K : K + 2 * L, K:] = 1
    bf16 = lambda a: np.asarray(a, np.float32).astype(ml_dtypes.bfloat16)
    f32 = lambda a: np.asarray(a, np.float32)
    mats = [bf16(major), bf16(minor), bf16(lanes), bf16(pack), bf16(pick), f32(keep), bf16(spread), f32(keep_z), bf16(fill)]
    return diagonal, mats


def dot(a, b):
    return jnp.dot(a, b, preferred_element_type=jnp.float32)


def lanes3(parts):
    return jnp.concatenate(parts, axis=1)


def turn(value, shift):
    return pltpu.roll(value, shift, axis=1)


def kernel(
    diagonal,
    blocks, fields, trial, major, minor, lanes, pack, pick, keep, spread, keep_z, fill,
    handed, projection,
    w_in, s1, y1, t1, t2, s2, x2, out_v, trial_v, fx_s, fx_r, fy_s, fy_r, fy, c1, c2,
    prod, p_s, p_r, q_s, q_r,
    z_send, z_recv, s1_send, y1_recv, s2_send, x2_recv, o_send, o_recv, tr_sem,
    fx_sem, fy_sem, ff_sem, p_sem, q_sem,
):
    bf16 = jnp.bfloat16
    tm = lax.axis_index("tm")
    sp = lax.axis_index("space")
    odd = lax.rem(tm, 2)
    even = odd == 0
    up = lax.rem(tm + 2, TM)
    down = lax.rem(tm + TM - 2, TM)
    beside = lax.rem(tm + TM - 1 + 2 * odd, TM)
    my_y = sp // GRID
    my_x = lax.rem(sp, GRID)
    cube = diagonal**3

    def peer(k):
        return lax.rem(my_y + k // GRID, GRID) * GRID + lax.rem(my_x + lax.rem(k, GRID), GRID)

    def remote(src, dst, send, recv, device):
        return pltpu.make_async_remote_copy(
            src_ref=src, dst_ref=dst, send_sem=send, recv_sem=recv, device_id=device, device_id_type=MESH
        )

    def to_peers(copy):
        @pl.loop(1, SPACE)
        def _(k):
            copy(peer(k))

    def arrived(ref, sem):
        pltpu.make_async_copy(ref, ref, sem).wait()

    barrier = pltpu.get_barrier_semaphore()

    def greet(device):
        pl.semaphore_signal(barrier, inc=1, device_id=device, device_id_type=MESH)

    to_peers(lambda j: greet((tm, j)))
    for other in (up, down, beside):
        greet((other, sp))
    pl.semaphore_wait(barrier, SPACE + 2)

    def hand(g):
        for x in range(R):
            remote(
                blocks.at[x, :, pl.ds(g * ZS, ZS), :], w_in.at[g, x], z_send.at[g], z_recv.at[g], (up, sp)
            ).start()

    @pl.when(even)
    def _():
        hand(0)
        hand(1)

    @pl.when(odd == 1)
    def _():
        for g in range(G):
            for x in range(R):
                pltpu.make_async_copy(blocks.at[x, :, pl.ds(g * ZS, ZS), :], w_in.at[g, x], z_recv.at[g]).start()

    lane = lax.broadcasted_iota(jnp.int32, (1, 3 * L), 1)
    scale = jnp.where(lane < L, cube * MIX_SCALAR, cube * MIX_ISOSPIN)
    scaled = (fields[...].reshape(R * L, 3 * L) * scale).astype(bf16)
    placed = dot(scaled, lanes[...]).astype(bf16)
    fx_s[0] = placed[:, :K].reshape(R, L, K)
    fx_s[1] = placed[:, K : 2 * K].reshape(R, L, K)
    stacked = jnp.concatenate([placed[:, :K], placed[:, K : 2 * K], placed[:, 2 * K :]], axis=0)
    fy_s[...] = dot(pack[...], stacked).astype(bf16).reshape(SPACE, 16, K)
    fy_r[sp] = fy_s[sp]
    remote(fx_s, fx_r, fx_sem.at[0], fx_sem.at[1], (beside, sp)).start()
    to_peers(lambda j: remote(fy_s.at[j], fy_r.at[sp], fy_sem.at[0], fy_sem.at[1], (tm, j)).start())

    for g in range(G):
        for x in range(R):
            pltpu.make_async_copy(trial.at[x, :, pl.ds(g * ZS, ZS), :], trial_v.at[g, x], tr_sem).start()

    @pl.when(even)
    def _():
        arrived(fy_r.at[pl.ds(0, SPACE - 1)], fy_sem.at[1])
        remote(fy_r, fy, ff_sem.at[0], ff_sem.at[1], (up, sp)).start()

    def coefficients():
        @pl.when(even)
        def _():
            arrived(fy, ff_sem.at[1])

        @pl.when(odd == 1)
        def _():
            arrived(fy_r.at[pl.ds(0, SPACE - 1)], fy_sem.at[1])
            fy[...] = fy_r[...]

        top = lax.broadcasted_iota(jnp.int32, (1, 2 * K), 1)
        constant = jnp.where(top < K, cube, 0.0)

        @pl.loop(0, SPACE)
        def _(i):
            rows = (dot(pick[...], fy[i]) * keep[...]).astype(bf16)
            both = lanes3([rows[: R * TRI], rows[R * TRI :]])
            c1[i] = dot(both, fill[...]) + constant

        arrived(fx_r, fx_sem.at[1])

        @pl.loop(0, R)
        def _(x):
            rows = dot(spread[...], lanes3([fx_r[0, x], fx_r[1, x]])).reshape(L, ZS, 2 * K)
            for g in range(G):
                mine = (rows * keep_z[g][None]).reshape(ROWS, 2 * K).astype(bf16)
                c2[g, x] = dot(mine, fill[...]) + constant

    @pl.loop(0, G + 1)
    def _(t):
        @pl.when(t < G)
        def _():
            g = t
            arrived(w_in.at[g], z_recv.at[g])

            @pl.when(jnp.logical_and(even, g == 0))
            def _():
                hand(2)

            moved = dot(major[...], lanes3([w_in[g, x].reshape(ROWS, K) for x in range(R)])).astype(bf16)
            for x in range(R):
                s1[g, x] = moved[:, x * K : (x + 1) * K].reshape(L, ZS, K)
            y1[g, pl.ds(sp * R, R)] = s1[g, :, pl.ds(sp * R, R)]
            to_peers(
                lambda j: remote(
                    s1.at[g, :, pl.ds(j * R, R)], y1.at[g, pl.ds(sp * R, R)], s1_send.at[g], y1_recv.at[g], (tm, j)
                ).start()
            )

        @pl.when(t == 1)
        def _():
            coefficients()

        @pl.when(t > 0)
        def _():
            g = t - 1
            arrived(y1.at[g, pl.ds(0, L - R)], y1_recv.at[g])
            moved = dot(major[...], lanes3([y1[g, :, y].reshape(ROWS, K) for y in range(R)])).astype(bf16)
            for y in range(R):
                t1[g, y] = moved[:, y * K : (y + 1) * K].reshape(L, ZS, K)

    @pl.loop(0, SPACE)
    def _(i):
        def column(y):
            return jnp.concatenate([t1[g, y, pl.ds(i * R, R)].reshape(R * ZS, K) for g in range(G)], axis=0)

        moved = dot(minor[...], lanes3([column(y) for y in range(R)]))
        mixed = []
        for y in range(R):
            own = moved[:, y * K : (y + 1) * K]
            coefs = c1[i, y * TRI : (y + 1) * TRI]
            mixed.append((coefs[:, :K] * own + coefs[:, K:] * turn(own, K // 2)).astype(bf16))
        again = dot(minor[...], lanes3(mixed)).astype(bf16)
        for y in range(R):
            for g in range(G):
                t2[g, y, pl.ds(i * R, R)] = again[
                    g * R * ZS : (g + 1) * R * ZS, y * K : (y + 1) * K
                ].reshape(R, ZS, K)

    @pl.loop(0, G)
    def _(g):
        moved = dot(major[...], lanes3([t2[g, y].reshape(ROWS, K) for y in range(R)])).astype(bf16)
        for y in range(R):
            s2[g, :, y] = moved[:, y * K : (y + 1) * K].reshape(L, ZS, K)
        x2[g, :, pl.ds(sp * R, R)] = s2[g, pl.ds(sp * R, R)]
        to_peers(
            lambda j: remote(
                s2.at[g, pl.ds(j * R, R)], x2.at[g, :, pl.ds(sp * R, R)], s2_send.at[g], x2_recv.at[g], (tm, j)
            ).start()
        )

    prod[...] = jnp.zeros_like(prod)
    arrived(trial_v, tr_sem)

    @pl.loop(0, G)
    def _(g):
        arrived(x2.at[g, :, pl.ds(0, L - R)], x2_recv.at[g])
        moved = dot(major[...], lanes3([x2[g, x].reshape(ROWS, K) for x in range(R)]))
        for x in range(R):
            own = moved[:, x * K : (x + 1) * K]
            coefs = c2[g, x]
            mixed = (coefs[:, :K] * own + coefs[:, K:] * turn(own, K // 2)).astype(bf16)
            out_v[g, x] = mixed.reshape(L, ZS, K)
            target = handed.at[x, :, pl.ds(g * ZS, ZS), :]

            @pl.when(even)
            def _():
                pltpu.make_async_copy(out_v.at[g, x], target, o_recv).start()

            @pl.when(odd == 1)
            def _():
                remote(out_v.at[g, x], target, o_send, o_recv, (up, sp)).start()

            prod[...] += lax.dot_general(
                trial_v[g, x].reshape(ROWS, K), mixed, (((0,), (0,)), ((), ())), preferred_element_type=jnp.float32
            )

    total = prod[:ORB]
    for c in range(1, C4):
        total = total + turn(prod[c * ORB : (c + 1) * ORB], K - c * ORB)
    quarter = lax.broadcasted_iota(jnp.int32, (8, K), 1) // ORB
    packed = jnp.where(quarter == 0, total[:8], 0.0)
    for q in range(1, 4):
        packed = packed + jnp.where(quarter == q, turn(total[8 * q : 8 * q + 8], q * ORB), 0.0)
    p_s[...] = packed
    p_r[sp] = packed
    to_peers(lambda j: remote(p_s, p_r.at[sp], p_sem.at[0], p_sem.at[1], (tm, j)).start())
    arrived(p_r.at[pl.ds(0, SPACE - 1)], p_sem.at[1])
    q_s[...] = jnp.sum(p_r[...], axis=0) * (1.0 / math.sqrt(C4 * L**3))

    @pl.when(even)
    def _():
        remote(q_s, q_r, q_sem.at[0], q_sem.at[1], (down, sp)).start()
        arrived(q_r, q_sem.at[1])

    @pl.when(odd == 1)
    def _():
        q_r[...] = q_s[...]

    result = q_r[...]
    for q in range(4):
        rows = result if q == 0 else turn(result, K - q * ORB)
        projection[8 * q : 8 * q + 8, :] = rows[:, :ORB]

    arrived(fx_s, fx_sem.at[0])
    arrived(fy_s.at[pl.ds(0, SPACE - 1)], fy_sem.at[0])
    arrived(p_r.at[pl.ds(0, SPACE - 1)], p_sem.at[0])
    for g in range(G):
        arrived(s1.at[g, :, pl.ds(0, L - R)], s1_send.at[g])
        arrived(s2.at[g, pl.ds(0, L - R)], s2_send.at[g])

    @pl.when(even)
    def _():
        for g in range(G):
            arrived(w_in.at[g], z_send.at[g])
        arrived(fy_r, ff_sem.at[0])
        arrived(q_s, q_sem.at[0])

    @pl.when(odd == 1)
    def _():
        arrived(out_v, o_send)

    arrived(out_v, o_recv)


def body(blocks, fields, trial):
    diagonal, mats = tables()
    bf16, f32 = jnp.bfloat16, jnp.float32
    vmem = pl.BlockSpec(memory_space=pltpu.VMEM)
    hbm = pl.BlockSpec(memory_space=pl.ANY)
    dma = pltpu.SemaphoreType.DMA
    by_x = pltpu.VMEM((G, R, L, ZS, K), bf16)
    by_pair = pltpu.VMEM((G, L, R, ZS, K), bf16)
    packed = pltpu.VMEM((SPACE, 16, K), bf16)
    tile = pltpu.VMEM((8, K), f32)
    scratch = [
        by_x, by_x, by_pair, by_x, by_x, by_pair, by_x, by_x, by_x,
        pltpu.VMEM((2, R, L, K), bf16), pltpu.VMEM((2, R, L, K), bf16),
        packed, packed, packed,
        pltpu.VMEM((SPACE, R * TRI, 2 * K), f32), pltpu.VMEM((G, R, ROWS, 2 * K), f32),
        pltpu.VMEM((K, K), f32), tile, pltpu.VMEM((SPACE, 8, K), f32), tile, tile,
        dma((G,)), dma((G,)), dma((G,)), dma((G,)), dma((G,)), dma((G,)), dma(()), dma(()), dma(()),
        dma((2,)), dma((2,)), dma((2,)), dma((2,)), dma((2,)),
    ]
    return pl.pallas_call(
        lambda *refs: kernel(diagonal, *refs),
        out_shape=(
            jax.ShapeDtypeStruct(blocks.shape, bf16),
            jax.ShapeDtypeStruct((ORB, ORB), f32),
        ),
        in_specs=[hbm, vmem, hbm] + [vmem] * len(mats),
        out_specs=(hbm, vmem),
        scratch_shapes=scratch,
        compiler_params=pltpu.CompilerParams(
            collective_id=0, has_side_effects=True, vmem_limit_bytes=56 * 1024 * 1024
        ),
    )(blocks, fields, trial, *[jnp.asarray(m) for m in mats])


def solution(mesh):
    in_specs = (
        P(("tm", "space"), None, None, None),
        P(("tm", "space"), None, None),
        P("space", None, None, None),
    )
    out_specs = (P(("tm", "space"), None, None, None), P("tm", None))
    return jax.shard_map(body, mesh=mesh, in_specs=in_specs, out_specs=out_specs, check_vma=False)
```

time: 331 us -> 89.3 us (0.27)
  the two profiles are of different devices: /device:TPU:1 before, /device:TPU:4 now
where the time goes in v1:
time: 89.3 us; the launch traced here: 89.1 us
  Pallas kernels  84.9 us (95%)
  local copies, waits for them, and re-layouts  3.6 us (4%)
    pallas_call x1, Pallas kernels, body(): pl.pallas_call(lambda *refs: kernel(diagonal, *refs), out_shape=(jax.Shap...  84.9 us
    unnamed x4, local copies, waits for them, and re-layouts  3.6 us

profile of v1, /device:TPU:4, one launch (start us, length us, event | category | flops | bytes accessed | tf_op | source)
XLA Modules:
  0.0 89.1 jit_solution(2642686534066736487)
XLA Ops:
  0.6 84.9 %shard_map.131 = (bf16[3,48,48,128]{3,2,1,0:T(8,128)(2,1)}, f32[32,32]{1,0:T(8,128)}) custom-call(bf16[3,48,48,128]{3,2,1,0:T(8,128)(2,1)} %refs_0_.1, f32[3,48,144]{2,1,0:T(8,128)} %refs_1_.1, bf16[3,48,48,128]{3,2,1,0:T(8,128)(2,1)} %refs_2_.1, bf16[768,768]{1,0:T(8,128)(2,1)} %constant.18.clone.refs_3_, bf16[144,144]{1,0:T(8,128)(2,1)} %constant.19.clone.refs_4_, ...), custom_call_target="tpu_custom_call" | custom-call | tf_op jit(solution)/shard_map/pallas_call | solution.py:368
  85.5 0.0 copy-start
  85.5 3.0 %copy.16 = bf16[3,48,48,128]{3,2,1,0:T(8,128)(2,1)} copy(bf16[3,48,48,128]{3,2,1,0:T(8,128)(2,1)} %get-tuple-element.4) | data formatting | bytes 3538944
  88.5 0.0 copy-done
  88.5 0.6 copy.17
Async XLA Ops:
  85.5 3.0 %copy-start = (f32[32,32]{1,0:T(8,128)S(1)}, f32[32,32]{1,0:T(8,128)}, u32[]{:S(2)}) copy-start(f32[32,32]{1,0:T(8,128)} %get-tuple-element.5) | copy-start | bytes 12292

commit v2 on v1

--- a/solution.py
+++ b/solution.py
@@ -98,12 +98,13 @@
 
 def kernel(
     diagonal,
-    blocks, fields, trial, major, minor, lanes, pack, pick, keep, spread, keep_z, fill,
+    blocks, fields, trial, major_h, minor_h, lanes_h, pack_h, pick_h, keep_h, spread_h, keep_z_h, fill_h,
     handed, projection,
+    fields_v, major, minor, lanes, pack, pick, keep, spread, keep_z, fill,
     w_in, s1, y1, t1, t2, s2, x2, out_v, trial_v, fx_s, fx_r, fy_s, fy_r, fy, c1, c2,
     prod, p_s, p_r, q_s, q_r,
     z_send, z_recv, s1_send, y1_recv, s2_send, x2_recv, o_send, o_recv, tr_sem,
-    fx_sem, fy_sem, ff_sem, p_sem, q_sem,
+    fx_sem, fy_sem, ff_sem, p_sem, q_sem, in_sem,
 ):
     bf16 = jnp.bfloat16
     tm = lax.axis_index("tm")
@@ -133,26 +134,26 @@
     def arrived(ref, sem):
         pltpu.make_async_copy(ref, ref, sem).wait()
 
+    inputs = [
+        pltpu.make_async_copy(src, dst, in_sem.at[n])
+        for n, (src, dst) in enumerate(
+            zip(
+                (fields, lanes_h, pack_h, major_h, minor_h, pick_h, keep_h, spread_h, keep_z_h, fill_h),
+                (fields_v, lanes, pack, major, minor, pick, keep, spread, keep_z, fill),
+            )
+        )
+    ]
+    for copy in inputs:
+        copy.start()
+
     barrier = pltpu.get_barrier_semaphore()
 
     def greet(device):
         pl.semaphore_signal(barrier, inc=1, device_id=device, device_id_type=MESH)
 
-    to_peers(lambda j: greet((tm, j)))
     for other in (up, down, beside):
         greet((other, sp))
-    pl.semaphore_wait(barrier, SPACE + 2)
-
-    def hand(g):
-        for x in range(R):
-            remote(
-                blocks.at[x, :, pl.ds(g * ZS, ZS), :], w_in.at[g, x], z_send.at[g], z_recv.at[g], (up, sp)
-            ).start()
-
-    @pl.when(even)
-    def _():
-        hand(0)
-        hand(1)
+    to_peers(lambda j: greet((tm, j)))
 
     @pl.when(odd == 1)
     def _():
@@ -160,17 +161,33 @@
             for x in range(R):
                 pltpu.make_async_copy(blocks.at[x, :, pl.ds(g * ZS, ZS), :], w_in.at[g, x], z_recv.at[g]).start()
 
+    for copy in inputs:
+        copy.wait()
     lane = lax.broadcasted_iota(jnp.int32, (1, 3 * L), 1)
     scale = jnp.where(lane < L, cube * MIX_SCALAR, cube * MIX_ISOSPIN)
-    scaled = (fields[...].reshape(R * L, 3 * L) * scale).astype(bf16)
+    scaled = (fields_v[...].reshape(R * L, 3 * L) * scale).astype(bf16)
     placed = dot(scaled, lanes[...]).astype(bf16)
     fx_s[0] = placed[:, :K].reshape(R, L, K)
     fx_s[1] = placed[:, K : 2 * K].reshape(R, L, K)
     stacked = jnp.concatenate([placed[:, :K], placed[:, K : 2 * K], placed[:, 2 * K :]], axis=0)
     fy_s[...] = dot(pack[...], stacked).astype(bf16).reshape(SPACE, 16, K)
     fy_r[sp] = fy_s[sp]
+
+    pl.semaphore_wait(barrier, SPACE + 2)
+
+    def hand(g):
+        for x in range(R):
+            remote(
+                blocks.at[x, :, pl.ds(g * ZS, ZS), :], w_in.at[g, x], z_send.at[g], z_recv.at[g], (up, sp)
+            ).start()
+
+    @pl.when(even)
+    def _():
+        hand(0)
+        hand(1)
+
+    to_peers(lambda j: remote(fy_s.at[j], fy_r.at[sp], fy_sem.at[0], fy_sem.at[1], (tm, j)).start())
     remote(fx_s, fx_r, fx_sem.at[0], fx_sem.at[1], (beside, sp)).start()
-    to_peers(lambda j: remote(fy_s.at[j], fy_r.at[sp], fy_sem.at[0], fy_sem.at[1], (tm, j)).start())
 
     for g in range(G):
         for x in range(R):
@@ -198,7 +215,7 @@
         def _(i):
             rows = (dot(pick[...], fy[i]) * keep[...]).astype(bf16)
             both = lanes3([rows[: R * TRI], rows[R * TRI :]])
-            c1[i] = dot(both, fill[...]) + constant
+            c1[i] = (dot(both, fill[...]) + constant).reshape(R, TRI, 2 * K)
 
         arrived(fx_r, fx_sem.at[1])
 
@@ -209,75 +226,104 @@
                 mine = (rows * keep_z[g][None]).reshape(ROWS, 2 * K).astype(bf16)
                 c2[g, x] = dot(mine, fill[...]) + constant
 
-    @pl.loop(0, G + 1)
-    def _(t):
-        @pl.when(t < G)
-        def _():
-            g = t
-            arrived(w_in.at[g], z_recv.at[g])
-
-            @pl.when(jnp.logical_and(even, g == 0))
-            def _():
-                hand(2)
-
-            moved = dot(major[...], lanes3([w_in[g, x].reshape(ROWS, K) for x in range(R)])).astype(bf16)
-            for x in range(R):
-                s1[g, x] = moved[:, x * K : (x + 1) * K].reshape(L, ZS, K)
-            y1[g, pl.ds(sp * R, R)] = s1[g, :, pl.ds(sp * R, R)]
+    @pl.loop(0, G)
+    def _(g):
+        arrived(w_in.at[g], z_recv.at[g])
+
+        @pl.when(jnp.logical_and(even, g == 0))
+        def _():
+            hand(2)
+
+        moved = dot(major[...], lanes3([w_in[g, x].reshape(ROWS, K) for x in range(R)])).astype(bf16)
+        for x in range(R):
+            s1[g, x] = moved[:, x * K : (x + 1) * K].reshape(L, ZS, K)
+
+        @pl.when(g < G - 1)
+        def _():
             to_peers(
                 lambda j: remote(
                     s1.at[g, :, pl.ds(j * R, R)], y1.at[g, pl.ds(sp * R, R)], s1_send.at[g], y1_recv.at[g], (tm, j)
                 ).start()
             )
 
-        @pl.when(t == 1)
+        @pl.when(g == G - 1)
+        def _():
+            for y in range(R):
+                to_peers(
+                    lambda j: remote(
+                        s1.at[g, :, j * R + y], y1.at[g, pl.ds(sp * R, R), y], s1_send.at[g], y1_recv.at[g + y], (tm, j)
+                    ).start()
+                )
+
+        y1[g, pl.ds(sp * R, R)] = s1[g, :, pl.ds(sp * R, R)]
+
+        @pl.when(g == 2 * odd)
         def _():
             coefficients()
 
-        @pl.when(t > 0)
-        def _():
-            g = t - 1
-            arrived(y1.at[g, pl.ds(0, L - R)], y1_recv.at[g])
-            moved = dot(major[...], lanes3([y1[g, :, y].reshape(ROWS, K) for y in range(R)])).astype(bf16)
-            for y in range(R):
-                t1[g, y] = moved[:, y * K : (y + 1) * K].reshape(L, ZS, K)
-
-    @pl.loop(0, SPACE)
-    def _(i):
-        def column(y):
-            return jnp.concatenate([t1[g, y, pl.ds(i * R, R)].reshape(R * ZS, K) for g in range(G)], axis=0)
-
-        moved = dot(minor[...], lanes3([column(y) for y in range(R)]))
-        mixed = []
-        for y in range(R):
-            own = moved[:, y * K : (y + 1) * K]
-            coefs = c1[i, y * TRI : (y + 1) * TRI]
-            mixed.append((coefs[:, :K] * own + coefs[:, K:] * turn(own, K // 2)).astype(bf16))
-        again = dot(minor[...], lanes3(mixed)).astype(bf16)
-        for y in range(R):
+    @pl.loop(0, R)
+    def _(y):
+        @pl.when(y == 0)
+        def _():
+            for g in range(G - 1):
+                arrived(y1.at[g, pl.ds(0, L - R)], y1_recv.at[g])
+
+        arrived(y1.at[G - 1, pl.ds(0, L - R), y], y1_recv.at[G - 1 + y])
+        moved = dot(major[...], lanes3([y1[g, :, y].reshape(ROWS, K) for g in range(G)])).astype(bf16)
+        for g in range(G):
+            t1[g] = moved[:, g * K : (g + 1) * K].reshape(L, ZS, K)
+
+        def pair(n, carry):
+            def column(i):
+                return jnp.concatenate([t1[g, pl.ds(i * R, R)].reshape(R * ZS, K) for g in range(G)], axis=0)
+
+            both = dot(minor[...], lanes3([column(2 * n), column(2 * n + 1)]))
+            mixed = []
+            for m in range(2):
+                own = both[:, m * K : (m + 1) * K]
+                coefs = c1[2 * n + m, y]
+                mixed.append((coefs[:, :K] * own + coefs[:, K:] * turn(own, K // 2)).astype(bf16))
+            again = dot(minor[...], lanes3(mixed)).astype(bf16)
+            for m in range(2):
+                for g in range(G):
+                    t2[g, pl.ds((2 * n + m) * R, R)] = again[
+                        g * R * ZS : (g + 1) * R * ZS, m * K : (m + 1) * K
+                    ].reshape(R, ZS, K)
+            return carry
+
+        lax.fori_loop(0, SPACE // 2, pair, 0, unroll=4)
+
+        moved = dot(major[...], lanes3([t2[g].reshape(ROWS, K) for g in range(G)])).astype(bf16)
+        for g in range(G):
+            s2[y, g] = moved[:, g * K : (g + 1) * K].reshape(L, ZS, K)
+
+        @pl.when(y < R - 1)
+        def _():
+            to_peers(
+                lambda j: remote(
+                    s2.at[y, :, pl.ds(j * R, R)], x2.at[:, :, sp * R + y], s2_send.at[y], x2_recv.at[y], (tm, j)
+                ).start()
+            )
+
+        @pl.when(y == R - 1)
+        def _():
             for g in range(G):
-                t2[g, y, pl.ds(i * R, R)] = again[
-                    g * R * ZS : (g + 1) * R * ZS, y * K : (y + 1) * K
-                ].reshape(R, ZS, K)
+                to_peers(
+                    lambda j: remote(
+                        s2.at[y, g, pl.ds(j * R, R)], x2.at[g, :, sp * R + y], s2_send.at[y], x2_recv.at[y + g], (tm, j)
+                    ).start()
+                )
+
+        x2[:, :, sp * R + y] = s2[y, :, pl.ds(sp * R, R)]
+
+    prod[...] = jnp.zeros_like(prod)
+    arrived(trial_v, tr_sem)
+    for y in range(R - 1):
+        arrived(x2.at[:, :, pl.ds(0, SPACE - 1)], x2_recv.at[y])
 
     @pl.loop(0, G)
     def _(g):
-        moved = dot(major[...], lanes3([t2[g, y].reshape(ROWS, K) for y in range(R)])).astype(bf16)
-        for y in range(R):
-            s2[g, :, y] = moved[:, y * K : (y + 1) * K].reshape(L, ZS, K)
-        x2[g, :, pl.ds(sp * R, R)] = s2[g, pl.ds(sp * R, R)]
-        to_peers(
-            lambda j: remote(
-                s2.at[g, pl.ds(j * R, R)], x2.at[g, :, pl.ds(sp * R, R)], s2_send.at[g], x2_recv.at[g], (tm, j)
-            ).start()
-        )
-
-    prod[...] = jnp.zeros_like(prod)
-    arrived(trial_v, tr_sem)
-
-    @pl.loop(0, G)
-    def _(g):
-        arrived(x2.at[g, :, pl.ds(0, L - R)], x2_recv.at[g])
+        arrived(x2.at[g, :, pl.ds(0, SPACE - 1)], x2_recv.at[R - 1 + g])
         moved = dot(major[...], lanes3([x2[g, x].reshape(ROWS, K) for x in range(R)]))
         for x in range(R):
             own = moved[:, x * K : (x + 1) * K]
@@ -294,8 +340,12 @@
             def _():
                 remote(out_v.at[g, x], target, o_send, o_recv, (up, sp)).start()
 
+        for x in range(R):
             prod[...] += lax.dot_general(
-                trial_v[g, x].reshape(ROWS, K), mixed, (((0,), (0,)), ((), ())), preferred_element_type=jnp.float32
+                trial_v[g, x].reshape(ROWS, K),
+                out_v[g, x].reshape(ROWS, K),
+                (((0,), (0,)), ((), ())),
+                preferred_element_type=jnp.float32,
             )
 
     total = prod[:ORB]
@@ -330,7 +380,7 @@
     arrived(p_r.at[pl.ds(0, SPACE - 1)], p_sem.at[0])
     for g in range(G):
         arrived(s1.at[g, :, pl.ds(0, L - R)], s1_send.at[g])
-        arrived(s2.at[g, pl.ds(0, L - R)], s2_send.at[g])
+        arrived(s2.at[g, :, pl.ds(0, L - R)], s2_send.at[g])
 
     @pl.when(even)
     def _():
@@ -354,16 +404,18 @@
     dma = pltpu.SemaphoreType.DMA
     by_x = pltpu.VMEM((G, R, L, ZS, K), bf16)
     by_pair = pltpu.VMEM((G, L, R, ZS, K), bf16)
+    one_row = pltpu.VMEM((G, L, ZS, K), bf16)
     packed = pltpu.VMEM((SPACE, 16, K), bf16)
     tile = pltpu.VMEM((8, K), f32)
-    scratch = [
-        by_x, by_x, by_pair, by_x, by_x, by_pair, by_x, by_x, by_x,
+    scratch = [pltpu.VMEM(fields.shape, f32)] + [pltpu.VMEM(m.shape, m.dtype) for m in mats]
+    scratch += [
+        by_x, by_x, by_pair, one_row, one_row, by_x, by_x, by_x, by_x,
         pltpu.VMEM((2, R, L, K), bf16), pltpu.VMEM((2, R, L, K), bf16),
         packed, packed, packed,
-        pltpu.VMEM((SPACE, R * TRI, 2 * K), f32), pltpu.VMEM((G, R, ROWS, 2 * K), f32),
+        pltpu.VMEM((SPACE, R, TRI, 2 * K), f32), pltpu.VMEM((G, R, ROWS, 2 * K), f32),
         pltpu.VMEM((K, K), f32), tile, pltpu.VMEM((SPACE, 8, K), f32), tile, tile,
-        dma((G,)), dma((G,)), dma((G,)), dma((G,)), dma((G,)), dma((G,)), dma(()), dma(()), dma(()),
-        dma((2,)), dma((2,)), dma((2,)), dma((2,)), dma((2,)),
+        dma((G,)), dma((G,)), dma((G,)), dma((5,)), dma((G,)), dma((5,)), dma(()), dma(()), dma(()),
+        dma((2,)), dma((2,)), dma((2,)), dma((2,)), dma((2,)), dma((10,)),
     ]
     return pl.pallas_call(
         lambda *refs: kernel(diagonal, *refs),
@@ -371,7 +423,7 @@
             jax.ShapeDtypeStruct(blocks.shape, bf16),
             jax.ShapeDtypeStruct((ORB, ORB), f32),
         ),
-        in_specs=[hbm, vmem, hbm] + [vmem] * len(mats),
+        in_specs=[hbm] * (3 + len(mats)),
         out_specs=(hbm, vmem),
         scratch_shapes=scratch,
         compiler_params=pltpu.CompilerParams(

time: 89.3 us -> 80.4 us (0.900)
  the two profiles are of different devices: /device:TPU:4 before, /device:TPU:2 now
where the time goes in v2:
time: 80.4 us; the launch traced here: 80.2 us
  Pallas kernels  75.9 us (94%)
  local copies, waits for them, and re-layouts  3.6 us (4%)
    pallas_call x1, Pallas kernels, body(): pl.pallas_call(lambda *refs: kernel(diagonal, *refs), out_shape=(jax.Shap...  75.9 us
    unnamed x4, local copies, waits for them, and re-layouts  3.6 us

profile of v2, /device:TPU:2, one launch (start us, length us, event | category | flops | bytes accessed | tf_op | source)
XLA Modules:
  0.0 80.2 jit_solution(9208776792448109884)
XLA Ops:
  0.6 75.9 %shard_map.131 = (bf16[3,48,48,128]{3,2,1,0:T(8,128)(2,1)}, f32[32,32]{1,0:T(8,128)}) custom-call(bf16[3,48,48,128]{3,2,1,0:T(8,128)(2,1)} %refs_0_.1, f32[3,48,144]{2,1,0:T(8,128)} %refs_1_.1, bf16[3,48,48,128]{3,2,1,0:T(8,128)(2,1)} %refs_2_.1, bf16[768,768]{1,0:T(8,128)(2,1)} %constant.18.clone.refs_3_, bf16[144,144]{1,0:T(8,128)(2,1)} %constant.19.clone.refs_4_, ...), custom_call_target="tpu_custom_call" | custom-call | tf_op jit(solution)/shard_map/pallas_call | solution.py:420
  76.6 0.0 copy-start
  76.6 3.0 %copy.16 = bf16[3,48,48,128]{3,2,1,0:T(8,128)(2,1)} copy(bf16[3,48,48,128]{3,2,1,0:T(8,128)(2,1)} %get-tuple-element.4) | data formatting | bytes 3538944
  79.6 0.0 copy-done
  79.6 0.6 copy.17
Async XLA Ops:
  76.6 3.0 %copy-start = (f32[32,32]{1,0:T(8,128)S(1)}, f32[32,32]{1,0:T(8,128)}, u32[]{:S(2)}) copy-start(f32[32,32]{1,0:T(8,128)} %get-tuple-element.5) | copy-start | bytes 12292

commit v3 on v2

--- a/solution.py
+++ b/solution.py
@@ -101,9 +101,9 @@
     blocks, fields, trial, major_h, minor_h, lanes_h, pack_h, pick_h, keep_h, spread_h, keep_z_h, fill_h,
     handed, projection,
     fields_v, major, minor, lanes, pack, pick, keep, spread, keep_z, fill,
-    w_in, s1, y1, t1, t2, s2, x2, out_v, trial_v, fx_s, fx_r, fy_s, fy_r, fy, c1, c2,
+    w_in, s1, yh, y1, t1, t2, s2, x2, out_v, trial_v, trial_t, fx_s, fx_r, fy_s, fy_r, fy, c1, c2,
     prod, p_s, p_r, q_s, q_r,
-    z_send, z_recv, s1_send, y1_recv, s2_send, x2_recv, o_send, o_recv, tr_sem,
+    z_send, z_recv, h_recv, f_send, f_recv, s1_send, y1_recv, s2_send, x2_recv, o_send, o_recv, tr_sem,
     fx_sem, fy_sem, ff_sem, p_sem, q_sem, in_sem,
 ):
     bf16 = jnp.bfloat16
@@ -155,11 +155,16 @@
         greet((other, sp))
     to_peers(lambda j: greet((tm, j)))
 
+    def own(g):
+        for x in range(R):
+            pltpu.make_async_copy(blocks.at[x, :, pl.ds(g * ZS, ZS), :], w_in.at[g, x], z_recv.at[g]).start()
+
     @pl.when(odd == 1)
     def _():
-        for g in range(G):
-            for x in range(R):
-                pltpu.make_async_copy(blocks.at[x, :, pl.ds(g * ZS, ZS), :], w_in.at[g, x], z_recv.at[g]).start()
+        for g in range(G - 1):
+            own(g)
+
+    own(G - 1)
 
     for copy in inputs:
         copy.wait()
@@ -217,6 +222,13 @@
             both = lanes3([rows[: R * TRI], rows[R * TRI :]])
             c1[i] = (dot(both, fill[...]) + constant).reshape(R, TRI, 2 * K)
 
+        arrived(trial_v, tr_sem)
+
+        @pl.loop(0, G)
+        def _(g):
+            for x in range(R):
+                trial_t[g, :, x * ROWS : (x + 1) * ROWS] = jnp.transpose(trial_v[g, x].reshape(ROWS, K))
+
         arrived(fx_r, fx_sem.at[1])
 
         @pl.loop(0, R)
@@ -226,47 +238,81 @@
                 mine = (rows * keep_z[g][None]).reshape(ROWS, 2 * K).astype(bf16)
                 c2[g, x] = dot(mine, fill[...]) + constant
 
+    def onward(y):
+        remote(yh.at[:, y], y1.at[G - 1, :, y], f_send, f_recv.at[y], (up, sp)).start()
+
     @pl.loop(0, G)
-    def _(g):
+    def _(t):
+        g = lax.rem(t + (G - 1) * (1 - odd), G)
         arrived(w_in.at[g], z_recv.at[g])
 
-        @pl.when(jnp.logical_and(even, g == 0))
-        def _():
-            hand(2)
+        @pl.when(jnp.logical_and(even, t == G - 1))
+        def _():
+            onward(1)
+            onward(2)
 
         moved = dot(major[...], lanes3([w_in[g, x].reshape(ROWS, K) for x in range(R)])).astype(bf16)
         for x in range(R):
             s1[g, x] = moved[:, x * K : (x + 1) * K].reshape(L, ZS, K)
 
-        @pl.when(g < G - 1)
+        home = jnp.logical_and(even, t == 0)
+
+        @pl.when(home)
         def _():
             to_peers(
                 lambda j: remote(
-                    s1.at[g, :, pl.ds(j * R, R)], y1.at[g, pl.ds(sp * R, R)], s1_send.at[g], y1_recv.at[g], (tm, j)
+                    s1.at[g, :, pl.ds(j * R, R)], yh.at[pl.ds(sp * R, R)], s1_send.at[g], h_recv, (tm, j)
                 ).start()
             )
-
-        @pl.when(g == G - 1)
-        def _():
-            for y in range(R):
+            yh[pl.ds(sp * R, R)] = s1[g, :, pl.ds(sp * R, R)]
+
+        @pl.when(jnp.logical_not(home))
+        def _():
+            @pl.when(t < G - 1)
+            def _():
                 to_peers(
                     lambda j: remote(
-                        s1.at[g, :, j * R + y], y1.at[g, pl.ds(sp * R, R), y], s1_send.at[g], y1_recv.at[g + y], (tm, j)
+                        s1.at[g, :, pl.ds(j * R, R)], y1.at[g, pl.ds(sp * R, R)], s1_send.at[g], y1_recv.at[g], (tm, j)
                     ).start()
                 )
 
-        y1[g, pl.ds(sp * R, R)] = s1[g, :, pl.ds(sp * R, R)]
-
-        @pl.when(g == 2 * odd)
+            @pl.when(t == G - 1)
+            def _():
+                for y in range(R):
+                    to_peers(
+                        lambda j: remote(
+                            s1.at[g, :, j * R + y],
+                            y1.at[g, pl.ds(sp * R, R), y],
+                            s1_send.at[g],
+                            y1_recv.at[G - 1 + y],
+                            (tm, j),
+                        ).start()
+                    )
+
+            y1[g, pl.ds(sp * R, R)] = s1[g, :, pl.ds(sp * R, R)]
+
+        @pl.when(t == (G - 1) * odd)
         def _():
             coefficients()
+
+        @pl.when(jnp.logical_and(even, t == 1))
+        def _():
+            arrived(yh.at[pl.ds(0, L - R)], h_recv)
+            onward(0)
 
     @pl.loop(0, R)
     def _(y):
         @pl.when(y == 0)
         def _():
-            for g in range(G - 1):
-                arrived(y1.at[g, pl.ds(0, L - R)], y1_recv.at[g])
+            arrived(y1.at[0, pl.ds(0, L - R)], y1_recv.at[0])
+
+        @pl.when(jnp.logical_and(odd == 1, y == 0))
+        def _():
+            arrived(y1.at[1, pl.ds(0, L - R)], y1_recv.at[1])
+
+        @pl.when(even)
+        def _():
+            arrived(y1.at[G - 1, :, y], f_recv.at[y])
 
         arrived(y1.at[G - 1, pl.ds(0, L - R), y], y1_recv.at[G - 1 + y])
         moved = dot(major[...], lanes3([y1[g, :, y].reshape(ROWS, K) for g in range(G)])).astype(bf16)
@@ -317,7 +363,6 @@
         x2[:, :, sp * R + y] = s2[y, :, pl.ds(sp * R, R)]
 
     prod[...] = jnp.zeros_like(prod)
-    arrived(trial_v, tr_sem)
     for y in range(R - 1):
         arrived(x2.at[:, :, pl.ds(0, SPACE - 1)], x2_recv.at[y])
 
@@ -340,13 +385,7 @@
             def _():
                 remote(out_v.at[g, x], target, o_send, o_recv, (up, sp)).start()
 
-        for x in range(R):
-            prod[...] += lax.dot_general(
-                trial_v[g, x].reshape(ROWS, K),
-                out_v[g, x].reshape(ROWS, K),
-                (((0,), (0,)), ((), ())),
-                preferred_element_type=jnp.float32,
-            )
+        prod[...] += dot(trial_t[g], out_v[g].reshape(R * ROWS, K))
 
     total = prod[:ORB]
     for c in range(1, C4):
@@ -384,8 +423,9 @@
 
     @pl.when(even)
     def _():
-        for g in range(G):
+        for g in range(G - 1):
             arrived(w_in.at[g], z_send.at[g])
+        arrived(yh, f_send)
         arrived(fy_r, ff_sem.at[0])
         arrived(q_s, q_sem.at[0])
 
@@ -409,12 +449,13 @@
     tile = pltpu.VMEM((8, K), f32)
     scratch = [pltpu.VMEM(fields.shape, f32)] + [pltpu.VMEM(m.shape, m.dtype) for m in mats]
     scratch += [
-        by_x, by_x, by_pair, one_row, one_row, by_x, by_x, by_x, by_x,
+        by_x, by_x, pltpu.VMEM((L, R, ZS, K), bf16), by_pair, one_row, one_row, by_x, by_x, by_x, by_x,
+        pltpu.VMEM((G, K, R * ROWS), bf16),
         pltpu.VMEM((2, R, L, K), bf16), pltpu.VMEM((2, R, L, K), bf16),
         packed, packed, packed,
         pltpu.VMEM((SPACE, R, TRI, 2 * K), f32), pltpu.VMEM((G, R, ROWS, 2 * K), f32),
         pltpu.VMEM((K, K), f32), tile, pltpu.VMEM((SPACE, 8, K), f32), tile, tile,
-        dma((G,)), dma((G,)), dma((G,)), dma((5,)), dma((G,)), dma((5,)), dma(()), dma(()), dma(()),
+        dma((G,)), dma((G,)), dma(()), dma(()), dma((G,)), dma((G,)), dma((5,)), dma((G,)), dma((5,)), dma(()), dma(()), dma(()),
         dma((2,)), dma((2,)), dma((2,)), dma((2,)), dma((2,)), dma((10,)),
     ]
     return pl.pallas_call(

time: 80.4 us -> 81.6 us (1.015)
  the two profiles are of different devices: /device:TPU:2 before, /device:TPU:8 now
where the time goes in v3:
time: 81.6 us; the launch traced here: 81.4 us
  Pallas kernels  77.2 us (95%)
  local copies, waits for them, and re-layouts  3.6 us (4%)
    pallas_call x1, Pallas kernels, body(): pl.pallas_call(lambda *refs: kernel(diagonal, *refs), out_shape=(jax.Shap...  77.2 us
    unnamed x4, local copies, waits for them, and re-layouts  3.6 us

profile of v3, /device:TPU:8, one launch (start us, length us, event | category | flops | bytes accessed | tf_op | source)
XLA Modules:
  0.0 81.4 jit_solution(17679944421655211220)
XLA Ops:
  0.6 77.2 %shard_map.131 = (bf16[3,48,48,128]{3,2,1,0:T(8,128)(2,1)}, f32[32,32]{1,0:T(8,128)}) custom-call(bf16[3,48,48,128]{3,2,1,0:T(8,128)(2,1)} %refs_0_.1, f32[3,48,144]{2,1,0:T(8,128)} %refs_1_.1, bf16[3,48,48,128]{3,2,1,0:T(8,128)(2,1)} %refs_2_.1, bf16[768,768]{1,0:T(8,128)(2,1)} %constant.18.clone.refs_3_, bf16[144,144]{1,0:T(8,128)(2,1)} %constant.19.clone.refs_4_, ...), custom_call_target="tpu_custom_call" | custom-call | tf_op jit(solution)/shard_map/pallas_call | solution.py:461
  77.8 0.0 copy-start
  77.8 3.0 %copy.16 = bf16[3,48,48,128]{3,2,1,0:T(8,128)(2,1)} copy(bf16[3,48,48,128]{3,2,1,0:T(8,128)(2,1)} %get-tuple-element.4) | data formatting | bytes 3538944
  80.8 0.0 copy-done
  80.8 0.6 copy.17
Async XLA Ops:
  77.8 3.0 %copy-start = (f32[32,32]{1,0:T(8,128)S(1)}, f32[32,32]{1,0:T(8,128)}, u32[]{:S(2)}) copy-start(f32[32,32]{1,0:T(8,128)} %get-tuple-element.5) | copy-start | bytes 12292

commit v4 on v3

--- a/solution.py
+++ b/solution.py
@@ -27,6 +27,11 @@
 ROWS = L * ZS
 TRI = G * R * ZS
 MESH = pl.DeviceIdType.MESH
+ONE_HOP = [(0, 1), (1, 0), (0, 3), (3, 0), (1, 1), (3, 3), (1, 3), (3, 1)]
+TWO_HOPS = [
+    ((0, 1), (0, 1)), ((1, 0), (1, 0)), ((1, 1), (1, 1)),
+    ((0, 3), (1, 3)), ((0, 3), (3, 3)), ((3, 0), (3, 1)), ((3, 0), (3, 3)),
+]
 
 
 def tables():
@@ -101,9 +106,9 @@
     blocks, fields, trial, major_h, minor_h, lanes_h, pack_h, pick_h, keep_h, spread_h, keep_z_h, fill_h,
     handed, projection,
     fields_v, major, minor, lanes, pack, pick, keep, spread, keep_z, fill,
-    w_in, s1, yh, y1, t1, t2, s2, x2, out_v, trial_v, trial_t, fx_s, fx_r, fy_s, fy_r, fy, c1, c2,
+    w_in, s1, y1, t1, t2, s2, x2, out_v, trial_v, trial_t, st1, st1_y, st2, st2_g, fx_s, fx_r, fy_s, fy_r, fy, c1, c2,
     prod, p_s, p_r, q_s, q_r,
-    z_send, z_recv, h_recv, f_send, f_recv, s1_send, y1_recv, s2_send, x2_recv, o_send, o_recv, tr_sem,
+    z_send, z_recv, f_send, f_recv, s1_send, y1_recv, st1_recv, st1_send, st2_recv, st2_send, s2_send, x2_recv, o_send, o_recv, tr_sem,
     fx_sem, fy_sem, ff_sem, p_sem, q_sem, in_sem,
 ):
     bf16 = jnp.bfloat16
@@ -121,6 +126,9 @@
     def peer(k):
         return lax.rem(my_y + k // GRID, GRID) * GRID + lax.rem(my_x + lax.rem(k, GRID), GRID)
 
+    def at(offset):
+        return lax.rem(my_y + offset[0], GRID) * GRID + lax.rem(my_x + offset[1], GRID)
+
     def remote(src, dst, send, recv, device):
         return pltpu.make_async_remote_copy(
             src_ref=src, dst_ref=dst, send_sem=send, recv_sem=recv, device_id=device, device_id_type=MESH
@@ -130,6 +138,19 @@
         @pl.loop(1, SPACE)
         def _(k):
             copy(peer(k))
+
+    def exchange(source, target, stage, send, stage_sem, recv):
+        for n, (first, second) in enumerate(TWO_HOPS):
+            total = (first[0] + second[0], first[1] + second[1])
+            remote(source(at(total)), stage.at[n], send, stage_sem, (tm, at(first))).start()
+        for offset in ONE_HOP:
+            remote(source(at(offset)), target(sp), send, recv, (tm, at(offset))).start()
+
+    def forward(target, stage, stage_sem, send, recv):
+        arrived(stage, stage_sem)
+        for n, (first, second) in enumerate(TWO_HOPS):
+            origin = at((GRID - first[0], GRID - first[1]))
+            remote(stage.at[n], target(origin), send, recv, (tm, at(second))).start()
 
     def arrived(ref, sem):
         pltpu.make_async_copy(ref, ref, sem).wait()
@@ -222,6 +243,10 @@
             both = lanes3([rows[: R * TRI], rows[R * TRI :]])
             c1[i] = (dot(both, fill[...]) + constant).reshape(R, TRI, 2 * K)
 
+        @pl.when(odd == 1)
+        def _():
+            forward_rows()
+
         arrived(trial_v, tr_sem)
 
         @pl.loop(0, G)
@@ -239,11 +264,39 @@
                 c2[g, x] = dot(mine, fill[...]) + constant
 
     def onward(y):
-        remote(yh.at[:, y], y1.at[G - 1, :, y], f_send, f_recv.at[y], (up, sp)).start()
+        remote(y1.at[G, :, y], y1.at[G - 1, :, y], f_send, f_recv.at[y], (up, sp)).start()
+
+    def place(t):
+        return jnp.where(even, lax.rem(t + G, G + 1), t)
+
+    def forward_whole(t):
+        q = place(t)
+        forward(lambda i: y1.at[q, pl.ds(i * R, R)], st1.at[t], st1_recv.at[t], st1_send.at[t], y1_recv.at[q])
+
+    def forward_rows():
+        q = jnp.where(even, 1, 2)
+
+        @pl.loop(0, R)
+        def _(y):
+            forward(
+                lambda i: y1.at[q, pl.ds(i * R, R), y],
+                st1_y.at[y], st1_recv.at[2 + y], st1_send.at[2 + y], y1_recv.at[4 + y],
+            )
 
     @pl.loop(0, G)
     def _(t):
         g = lax.rem(t + (G - 1) * (1 - odd), G)
+        q = place(t)
+
+        @pl.when(jnp.logical_and(even, t > 0))
+        def _():
+            forward_whole(t - 1)
+
+        @pl.when(jnp.logical_and(even, t == 1))
+        def _():
+            arrived(y1.at[G, pl.ds(0, L - R)], y1_recv.at[G])
+            onward(0)
+
         arrived(w_in.at[g], z_recv.at[g])
 
         @pl.when(jnp.logical_and(even, t == G - 1))
@@ -255,50 +308,37 @@
         for x in range(R):
             s1[g, x] = moved[:, x * K : (x + 1) * K].reshape(L, ZS, K)
 
-        home = jnp.logical_and(even, t == 0)
-
-        @pl.when(home)
-        def _():
-            to_peers(
-                lambda j: remote(
-                    s1.at[g, :, pl.ds(j * R, R)], yh.at[pl.ds(sp * R, R)], s1_send.at[g], h_recv, (tm, j)
-                ).start()
+        @pl.when(t < G - 1)
+        def _():
+            exchange(
+                lambda j: s1.at[g, :, pl.ds(j * R, R)],
+                lambda i: y1.at[q, pl.ds(i * R, R)],
+                st1.at[t], s1_send.at[g], st1_recv.at[t], y1_recv.at[q],
             )
-            yh[pl.ds(sp * R, R)] = s1[g, :, pl.ds(sp * R, R)]
-
-        @pl.when(jnp.logical_not(home))
-        def _():
-            @pl.when(t < G - 1)
-            def _():
-                to_peers(
-                    lambda j: remote(
-                        s1.at[g, :, pl.ds(j * R, R)], y1.at[g, pl.ds(sp * R, R)], s1_send.at[g], y1_recv.at[g], (tm, j)
-                    ).start()
+
+        @pl.when(t == G - 1)
+        def _():
+            @pl.loop(0, R)
+            def _(y):
+                exchange(
+                    lambda j: s1.at[g, :, j * R + y],
+                    lambda i: y1.at[q, pl.ds(i * R, R), y],
+                    st1_y.at[y], s1_send.at[g], st1_recv.at[2 + y], y1_recv.at[4 + y],
                 )
 
-            @pl.when(t == G - 1)
-            def _():
-                for y in range(R):
-                    to_peers(
-                        lambda j: remote(
-                            s1.at[g, :, j * R + y],
-                            y1.at[g, pl.ds(sp * R, R), y],
-                            s1_send.at[g],
-                            y1_recv.at[G - 1 + y],
-                            (tm, j),
-                        ).start()
-                    )
-
-            y1[g, pl.ds(sp * R, R)] = s1[g, :, pl.ds(sp * R, R)]
+        y1[q, pl.ds(sp * R, R)] = s1[g, :, pl.ds(sp * R, R)]
+
+        @pl.when(jnp.logical_and(odd == 1, t > 0))
+        def _():
+            forward_whole(t - 1)
 
         @pl.when(t == (G - 1) * odd)
         def _():
             coefficients()
 
-        @pl.when(jnp.logical_and(even, t == 1))
-        def _():
-            arrived(yh.at[pl.ds(0, L - R)], h_recv)
-            onward(0)
+    @pl.when(even)
+    def _():
+        forward_rows()
 
     @pl.loop(0, R)
     def _(y):
@@ -314,7 +354,7 @@
         def _():
             arrived(y1.at[G - 1, :, y], f_recv.at[y])
 
-        arrived(y1.at[G - 1, pl.ds(0, L - R), y], y1_recv.at[G - 1 + y])
+        arrived(y1.at[G - 1, pl.ds(0, L - R), y], y1_recv.at[4 + y])
         moved = dot(major[...], lanes3([y1[g, :, y].reshape(ROWS, K) for g in range(G)])).astype(bf16)
         for g in range(G):
             t1[g] = moved[:, g * K : (g + 1) * K].reshape(L, ZS, K)
@@ -345,22 +385,37 @@
 
         @pl.when(y < R - 1)
         def _():
-            to_peers(
-                lambda j: remote(
-                    s2.at[y, :, pl.ds(j * R, R)], x2.at[:, :, sp * R + y], s2_send.at[y], x2_recv.at[y], (tm, j)
-                ).start()
+            exchange(
+                lambda j: s2.at[y, :, pl.ds(j * R, R)],
+                lambda i: x2.at[:, :, i * R + y],
+                st2.at[y], s2_send.at[y], st2_recv.at[y], x2_recv.at[y],
             )
 
         @pl.when(y == R - 1)
         def _():
-            for g in range(G):
-                to_peers(
-                    lambda j: remote(
-                        s2.at[y, g, pl.ds(j * R, R)], x2.at[g, :, sp * R + y], s2_send.at[y], x2_recv.at[y + g], (tm, j)
-                    ).start()
+            @pl.loop(0, G)
+            def _(g):
+                exchange(
+                    lambda j: s2.at[y, g, pl.ds(j * R, R)],
+                    lambda i: x2.at[g, :, i * R + y],
+                    st2_g.at[g], s2_send.at[y], st2_recv.at[2 + g], x2_recv.at[2 + g],
                 )
 
         x2[:, :, sp * R + y] = s2[y, :, pl.ds(sp * R, R)]
+
+        @pl.when(y > 0)
+        def _():
+            forward(
+                lambda i: x2.at[:, :, i * R + y - 1],
+                st2.at[y - 1], st2_recv.at[y - 1], st2_send.at[y - 1], x2_recv.at[y - 1],
+            )
+
+    @pl.loop(0, G)
+    def _(g):
+        forward(
+            lambda i: x2.at[g, :, i * R + R - 1],
+            st2_g.at[g], st2_recv.at[2 + g], st2_send.at[2 + g], x2_recv.at[2 + g],
+        )
 
     prod[...] = jnp.zeros_like(prod)
     for y in range(R - 1):
@@ -425,9 +480,16 @@
     def _():
         for g in range(G - 1):
             arrived(w_in.at[g], z_send.at[g])
-        arrived(yh, f_send)
+        arrived(y1.at[G], f_send)
         arrived(fy_r, ff_sem.at[0])
         arrived(q_s, q_sem.at[0])
+
+    for t in range(2):
+        arrived(st1.at[t], st1_send.at[t])
+        arrived(st2.at[t], st2_send.at[t])
+    for n in range(3):
+        arrived(st1_y.at[n], st1_send.at[2 + n])
+        arrived(st2_g.at[n], st2_send.at[2 + n])
 
     @pl.when(odd == 1)
     def _():
@@ -443,19 +505,20 @@
     hbm = pl.BlockSpec(memory_space=pl.ANY)
     dma = pltpu.SemaphoreType.DMA
     by_x = pltpu.VMEM((G, R, L, ZS, K), bf16)
-    by_pair = pltpu.VMEM((G, L, R, ZS, K), bf16)
     one_row = pltpu.VMEM((G, L, ZS, K), bf16)
     packed = pltpu.VMEM((SPACE, 16, K), bf16)
     tile = pltpu.VMEM((8, K), f32)
     scratch = [pltpu.VMEM(fields.shape, f32)] + [pltpu.VMEM(m.shape, m.dtype) for m in mats]
     scratch += [
-        by_x, by_x, pltpu.VMEM((L, R, ZS, K), bf16), by_pair, one_row, one_row, by_x, by_x, by_x, by_x,
+        by_x, by_x, pltpu.VMEM((G + 1, L, R, ZS, K), bf16), one_row, one_row, by_x, by_x, by_x, by_x,
         pltpu.VMEM((G, K, R * ROWS), bf16),
+        pltpu.VMEM((2, 7, R, R, ZS, K), bf16), pltpu.VMEM((R, 7, R, ZS, K), bf16),
+        pltpu.VMEM((2, 7, G, R, ZS, K), bf16), pltpu.VMEM((G, 7, R, ZS, K), bf16),
         pltpu.VMEM((2, R, L, K), bf16), pltpu.VMEM((2, R, L, K), bf16),
         packed, packed, packed,
         pltpu.VMEM((SPACE, R, TRI, 2 * K), f32), pltpu.VMEM((G, R, ROWS, 2 * K), f32),
         pltpu.VMEM((K, K), f32), tile, pltpu.VMEM((SPACE, 8, K), f32), tile, tile,
-        dma((G,)), dma((G,)), dma(()), dma(()), dma((G,)), dma((G,)), dma((5,)), dma((G,)), dma((5,)), dma(()), dma(()), dma(()),
+        dma((G,)), dma((G,)), dma(()), dma((G,)), dma((G,)), dma((7,)), dma((5,)), dma((5,)), dma((5,)), dma((5,)), dma((G,)), dma((5,)), dma(()), dma(()), dma(()),
         dma((2,)), dma((2,)), dma((2,)), dma((2,)), dma((2,)), dma((10,)),
     ]
     return pl.pallas_call(

time: 81.6 us -> 96.3 us (1.18)
  the two profiles are of different devices: /device:TPU:8 before, /device:TPU:2 now
where the time goes in v4:
time: 96.3 us; the launch traced here: 96.2 us
  Pallas kernels  91.9 us (95%)
  local copies, waits for them, and re-layouts  3.6 us (4%)
    pallas_call x1, Pallas kernels, body(): pl.pallas_call(lambda *refs: kernel(diagonal, *refs), out_shape=(jax.Shap...  91.9 us
    unnamed x4, local copies, waits for them, and re-layouts  3.6 us

profile of v4, /device:TPU:2, one launch (start us, length us, event | category | flops | bytes accessed | tf_op | source)
XLA Modules:
  0.0 96.2 jit_solution(658170129589770768)
XLA Ops:
  0.6 91.9 %shard_map.131 = (bf16[3,48,48,128]{3,2,1,0:T(8,128)(2,1)}, f32[32,32]{1,0:T(8,128)}) custom-call(bf16[3,48,48,128]{3,2,1,0:T(8,128)(2,1)} %refs_0_.1, f32[3,48,144]{2,1,0:T(8,128)} %refs_1_.1, bf16[3,48,48,128]{3,2,1,0:T(8,128)(2,1)} %refs_2_.1, bf16[768,768]{1,0:T(8,128)(2,1)} %constant.18.clone.refs_3_, bf16[144,144]{1,0:T(8,128)(2,1)} %constant.19.clone.refs_4_, ...), custom_call_target="tpu_custom_call" | custom-call | tf_op jit(solution)/shard_map/pallas_call | solution.py:524
  92.5 0.0 copy-start
  92.6 3.0 %copy.16 = bf16[3,48,48,128]{3,2,1,0:T(8,128)(2,1)} copy(bf16[3,48,48,128]{3,2,1,0:T(8,128)(2,1)} %get-tuple-element.4) | data formatting | bytes 3538944
  95.6 0.0 copy-done
  95.6 0.6 copy.17
Async XLA Ops:
  92.5 3.0 %copy-start = (f32[32,32]{1,0:T(8,128)S(1)}, f32[32,32]{1,0:T(8,128)}, u32[]{:S(2)}) copy-start(f32[32,32]{1,0:T(8,128)} %get-tuple-element.5) | copy-start | bytes 12292

commit v5 on v3

--- a/solution.py
+++ b/solution.py
@@ -55,19 +55,12 @@
                 pack[j, n, 0, x, R * j + y] = 1
                 pack[j, 9 + n // 2, 1 + n % 2, x, R * j + y] = 1
     pack = pack.reshape(SPACE * 16, 3 * R * L)
-    pick = np.zeros((2, R, G, R, ZS, 16))
-    keep = np.zeros((2, R, G, R, ZS, K))
-    for y in range(R):
-        for x in range(R):
-            n = x * R + y
-            pick[0, y, :, x, :, n] = 1
-            pick[1, y, :, x, :, 9 + n // 2] = 1
-            for g in range(G):
-                for z in range(ZS):
-                    keep[0, y, g, x, z, [ZS * g + z, L + ZS * g + z]] = 1
-                    keep[1, y, g, x, z, L * (n % 2) + ZS * g + z] = 1
-    pick = pick.reshape(2 * R * TRI, 16)
-    keep = keep.reshape(2 * R * TRI, K)
+    keep = np.zeros((3, G, ZS, K))
+    for g in range(G):
+        for z in range(ZS):
+            keep[0, g, z, [ZS * g + z, L + ZS * g + z]] = 1
+            keep[1, g, z, ZS * g + z] = 1
+            keep[2, g, z, L + ZS * g + z] = 1
     spread = np.kron(np.eye(L), np.ones((ZS, 1)))
     keep_z = np.zeros((G, ZS, 2 * K))
     for g in range(G):
@@ -80,7 +73,7 @@
     fill[K : K + 2 * L, K:] = 1
     bf16 = lambda a: np.asarray(a, np.float32).astype(ml_dtypes.bfloat16)
     f32 = lambda a: np.asarray(a, np.float32)
-    mats = [bf16(major), bf16(minor), bf16(lanes), bf16(pack), bf16(pick), f32(keep), bf16(spread), f32(keep_z), bf16(fill)]
+    mats = [bf16(major), bf16(minor), bf16(lanes), bf16(pack), f32(keep), bf16(spread), f32(keep_z), bf16(fill)]
     return diagonal, mats
 
 
@@ -98,9 +91,9 @@
 
 def kernel(
     diagonal,
-    blocks, fields, trial, major_h, minor_h, lanes_h, pack_h, pick_h, keep_h, spread_h, keep_z_h, fill_h,
+    blocks, fields, trial, major_h, minor_h, lanes_h, pack_h, keep_h, spread_h, keep_z_h, fill_h,
     handed, projection,
-    fields_v, major, minor, lanes, pack, pick, keep, spread, keep_z, fill,
+    fields_v, major, minor, lanes, pack, keep, spread, keep_z, fill,
     w_in, s1, yh, y1, t1, t2, s2, x2, out_v, trial_v, trial_t, fx_s, fx_r, fy_s, fy_r, fy, c1, c2,
     prod, p_s, p_r, q_s, q_r,
     z_send, z_recv, h_recv, f_send, f_recv, s1_send, y1_recv, s2_send, x2_recv, o_send, o_recv, tr_sem,
@@ -138,8 +131,8 @@
         pltpu.make_async_copy(src, dst, in_sem.at[n])
         for n, (src, dst) in enumerate(
             zip(
-                (fields, lanes_h, pack_h, major_h, minor_h, pick_h, keep_h, spread_h, keep_z_h, fill_h),
-                (fields_v, lanes, pack, major, minor, pick, keep, spread, keep_z, fill),
+                (fields, lanes_h, pack_h, major_h, minor_h, keep_h, spread_h, keep_z_h, fill_h),
+                (fields_v, lanes, pack, major, minor, keep, spread, keep_z, fill),
             )
         )
     ]
@@ -203,7 +196,10 @@
         arrived(fy_r.at[pl.ds(0, SPACE - 1)], fy_sem.at[1])
         remote(fy_r, fy, ff_sem.at[0], ff_sem.at[1], (up, sp)).start()
 
-    def coefficients():
+    top = lax.broadcasted_iota(jnp.int32, (1, 2 * K), 1)
+    constant = jnp.where(top < K, cube, 0.0)
+
+    def first_coefficients():
         @pl.when(even)
         def _():
             arrived(fy, ff_sem.at[1])
@@ -213,22 +209,24 @@
             arrived(fy_r.at[pl.ds(0, SPACE - 1)], fy_sem.at[1])
             fy[...] = fy_r[...]
 
-        top = lax.broadcasted_iota(jnp.int32, (1, 2 * K), 1)
-        constant = jnp.where(top < K, cube, 0.0)
-
-        @pl.loop(0, SPACE)
-        def _(i):
-            rows = (dot(pick[...], fy[i]) * keep[...]).astype(bf16)
-            both = lanes3([rows[: R * TRI], rows[R * TRI :]])
-            c1[i] = (dot(both, fill[...]) + constant).reshape(R, TRI, 2 * K)
-
-        arrived(trial_v, tr_sem)
-
-        @pl.loop(0, G)
-        def _(g):
-            for x in range(R):
-                trial_t[g, :, x * ROWS : (x + 1) * ROWS] = jnp.transpose(trial_v[g, x].reshape(ROWS, K))
-
+        def one(i, carry):
+            rows = fy[i].astype(jnp.float32)
+            both = []
+            for y in range(R):
+                diagonal_part, flip_part = [], []
+                for g in range(G):
+                    for x in range(R):
+                        n = x * R + y
+                        diagonal_part.append(rows[n : n + 1] * keep[0, g])
+                        flip_part.append(rows[9 + n // 2 : 10 + n // 2] * keep[1 + n % 2, g])
+                both.append(lanes3([jnp.concatenate(part, axis=0) for part in (diagonal_part, flip_part)]))
+            picked = jnp.concatenate(both, axis=0).astype(bf16)
+            c1[i] = (dot(picked, fill[...]) + constant).reshape(R, TRI, 2 * K)
+            return carry
+
+        lax.fori_loop(0, SPACE, one, 0, unroll=2)
+
+    def second_coefficients():
         arrived(fx_r, fx_sem.at[1])
 
         @pl.loop(0, R)
@@ -237,6 +235,17 @@
             for g in range(G):
                 mine = (rows * keep_z[g][None]).reshape(ROWS, 2 * K).astype(bf16)
                 c2[g, x] = dot(mine, fill[...]) + constant
+
+    def turn_trial():
+        arrived(trial_v, tr_sem)
+
+        @pl.loop(0, G)
+        def _(g):
+            for x in range(R):
+                trial_t[g, :, x * ROWS : (x + 1) * ROWS] = jnp.transpose(trial_v[g, x].reshape(ROWS, K))
+
+    def products(g):
+        prod[...] += dot(trial_t[g], out_v[g].reshape(R * ROWS, K))
 
     def onward(y):
         remote(yh.at[:, y], y1.at[G - 1, :, y], f_send, f_recv.at[y], (up, sp)).start()
@@ -291,9 +300,13 @@
 
             y1[g, pl.ds(sp * R, R)] = s1[g, :, pl.ds(sp * R, R)]
 
-        @pl.when(t == (G - 1) * odd)
-        def _():
-            coefficients()
+        @pl.when(home)
+        def _():
+            turn_trial()
+
+        @pl.when(t == 1 + odd)
+        def _():
+            first_coefficients()
 
         @pl.when(jnp.logical_and(even, t == 1))
         def _():
@@ -362,6 +375,7 @@
 
         x2[:, :, sp * R + y] = s2[y, :, pl.ds(sp * R, R)]
 
+    second_coefficients()
     prod[...] = jnp.zeros_like(prod)
     for y in range(R - 1):
         arrived(x2.at[:, :, pl.ds(0, SPACE - 1)], x2_recv.at[y])
@@ -385,7 +399,15 @@
             def _():
                 remote(out_v.at[g, x], target, o_send, o_recv, (up, sp)).start()
 
-        prod[...] += dot(trial_t[g], out_v[g].reshape(R * ROWS, K))
+        @pl.when(even)
+        def _():
+            products(g)
+
+    @pl.when(odd == 1)
+    def _():
+        turn_trial()
+        for g in range(G):
+            products(g)
 
     total = prod[:ORB]
     for c in range(1, C4):
@@ -456,7 +478,7 @@
         pltpu.VMEM((SPACE, R, TRI, 2 * K), f32), pltpu.VMEM((G, R, ROWS, 2 * K), f32),
         pltpu.VMEM((K, K), f32), tile, pltpu.VMEM((SPACE, 8, K), f32), tile, tile,
         dma((G,)), dma((G,)), dma(()), dma(()), dma((G,)), dma((G,)), dma((5,)), dma((G,)), dma((5,)), dma(()), dma(()), dma(()),
-        dma((2,)), dma((2,)), dma((2,)), dma((2,)), dma((2,)), dma((10,)),
+        dma((2,)), dma((2,)), dma((2,)), dma((2,)), dma((2,)), dma((9,)),
     ]
     return pl.pallas_call(
         lambda *refs: kernel(diagonal, *refs),

time: 81.6 us -> 74.2 us (0.909)
  the two profiles are of different devices: /device:TPU:8 before, /device:TPU:1 now
where the time goes in v5:
time: 74.2 us; the launch traced here: 74 us
  Pallas kernels  69.7 us (94%)
  local copies, waits for them, and re-layouts  3.6 us (5%)
    pallas_call x1, Pallas kernels, body(): pl.pallas_call(lambda *refs: kernel(diagonal, *refs), out_shape=(jax.Shap...  69.7 us
    unnamed x4, local copies, waits for them, and re-layouts  3.6 us

profile of v5, /device:TPU:1, one launch (start us, length us, event | category | flops | bytes accessed | tf_op | source)
XLA Modules:
  0.0 74.0 jit_solution(2825235235967548214)
XLA Ops:
  0.6 69.7 %shard_map.122 = (bf16[3,48,48,128]{3,2,1,0:T(8,128)(2,1)}, f32[32,32]{1,0:T(8,128)}) custom-call(bf16[3,48,48,128]{3,2,1,0:T(8,128)(2,1)} %refs_0_.1, f32[3,48,144]{2,1,0:T(8,128)} %refs_1_.1, bf16[3,48,48,128]{3,2,1,0:T(8,128)(2,1)} %refs_2_.1, bf16[768,768]{1,0:T(8,128)(2,1)} %constant.16.clone.refs_3_, bf16[144,144]{1,0:T(8,128)(2,1)} %constant.17.clone.refs_4_, ...), custom_call_target="tpu_custom_call" | custom-call | tf_op jit(solution)/shard_map/pallas_call | solution.py:483
  70.4 0.0 copy-start
  70.4 3.0 %copy.15 = bf16[3,48,48,128]{3,2,1,0:T(8,128)(2,1)} copy(bf16[3,48,48,128]{3,2,1,0:T(8,128)(2,1)} %get-tuple-element.4) | data formatting | bytes 3538944
  73.4 0.0 copy-done
  73.4 0.6 copy.16
Async XLA Ops:
  70.4 3.0 %copy-start = (f32[32,32]{1,0:T(8,128)S(1)}, f32[32,32]{1,0:T(8,128)}, u32[]{:S(2)}) copy-start(f32[32,32]{1,0:T(8,128)} %get-tuple-element.5) | copy-start | bytes 12292

commit v6 on v5

--- a/solution.py
+++ b/solution.py
@@ -95,9 +95,9 @@
     handed, projection,
     fields_v, major, minor, lanes, pack, keep, spread, keep_z, fill,
     w_in, s1, yh, y1, t1, t2, s2, x2, out_v, trial_v, trial_t, fx_s, fx_r, fy_s, fy_r, fy, c1, c2,
-    prod, p_s, p_r, q_s, q_r,
+    prod, p_s, p_r,
     z_send, z_recv, h_recv, f_send, f_recv, s1_send, y1_recv, s2_send, x2_recv, o_send, o_recv, tr_sem,
-    fx_sem, fy_sem, ff_sem, p_sem, q_sem, in_sem,
+    fx_sem, fy_sem, ff_sem, p_sem, in_sem,
 ):
     bf16 = jnp.bfloat16
     tm = lax.axis_index("tm")
@@ -112,17 +112,18 @@
     cube = diagonal**3
 
     def peer(k):
-        return lax.rem(my_y + k // GRID, GRID) * GRID + lax.rem(my_x + lax.rem(k, GRID), GRID)
+        return lax.rem(my_y + k // GRID, GRID) * GRID + lax.rem(my_x + k % GRID, GRID)
 
     def remote(src, dst, send, recv, device):
         return pltpu.make_async_remote_copy(
             src_ref=src, dst_ref=dst, send_sem=send, recv_sem=recv, device_id=device, device_id_type=MESH
         )
 
+    peers = [peer(k) for k in range(1, SPACE)]
+
     def to_peers(copy):
-        @pl.loop(1, SPACE)
-        def _(k):
-            copy(peer(k))
+        for j in peers:
+            copy(j)
 
     def arrived(ref, sem):
         pltpu.make_async_copy(ref, ref, sem).wait()
@@ -144,9 +145,19 @@
     def greet(device):
         pl.semaphore_signal(barrier, inc=1, device_id=device, device_id_type=MESH)
 
-    for other in (up, down, beside):
-        greet((other, sp))
+    greet((beside, sp))
     to_peers(lambda j: greet((tm, j)))
+
+    @pl.when(even)
+    def _():
+        for j in range(SPACE):
+            greet((up, j))
+            greet((down, j))
+
+    @pl.when(odd == 1)
+    def _():
+        greet((up, sp))
+        greet((down, sp))
 
     def own(g):
         for x in range(R):
@@ -159,19 +170,7 @@
 
     own(G - 1)
 
-    for copy in inputs:
-        copy.wait()
-    lane = lax.broadcasted_iota(jnp.int32, (1, 3 * L), 1)
-    scale = jnp.where(lane < L, cube * MIX_SCALAR, cube * MIX_ISOSPIN)
-    scaled = (fields_v[...].reshape(R * L, 3 * L) * scale).astype(bf16)
-    placed = dot(scaled, lanes[...]).astype(bf16)
-    fx_s[0] = placed[:, :K].reshape(R, L, K)
-    fx_s[1] = placed[:, K : 2 * K].reshape(R, L, K)
-    stacked = jnp.concatenate([placed[:, :K], placed[:, K : 2 * K], placed[:, 2 * K :]], axis=0)
-    fy_s[...] = dot(pack[...], stacked).astype(bf16).reshape(SPACE, 16, K)
-    fy_r[sp] = fy_s[sp]
-
-    pl.semaphore_wait(barrier, SPACE + 2)
+    pl.semaphore_wait(barrier, SPACE + 2 + 2 * (SPACE - 1) * (1 - odd))
 
     def hand(g):
         for x in range(R):
@@ -184,15 +183,27 @@
         hand(0)
         hand(1)
 
-    to_peers(lambda j: remote(fy_s.at[j], fy_r.at[sp], fy_sem.at[0], fy_sem.at[1], (tm, j)).start())
-    remote(fx_s, fx_r, fx_sem.at[0], fx_sem.at[1], (beside, sp)).start()
-
     for g in range(G):
         for x in range(R):
             pltpu.make_async_copy(trial.at[x, :, pl.ds(g * ZS, ZS), :], trial_v.at[g, x], tr_sem).start()
 
-    @pl.when(even)
-    def _():
+    for copy in inputs:
+        copy.wait()
+
+    def share_fields():
+        lane = lax.broadcasted_iota(jnp.int32, (1, 3 * L), 1)
+        scale = jnp.where(lane < L, cube * MIX_SCALAR, cube * MIX_ISOSPIN)
+        scaled = (fields_v[...].reshape(R * L, 3 * L) * scale).astype(bf16)
+        placed = dot(scaled, lanes[...]).astype(bf16)
+        fx_s[0] = placed[:, :K].reshape(R, L, K)
+        fx_s[1] = placed[:, K : 2 * K].reshape(R, L, K)
+        stacked = jnp.concatenate([placed[:, :K], placed[:, K : 2 * K], placed[:, 2 * K :]], axis=0)
+        fy_s[...] = dot(pack[...], stacked).astype(bf16).reshape(SPACE, 16, K)
+        fy_r[sp] = fy_s[sp]
+        to_peers(lambda j: remote(fy_s.at[j], fy_r.at[sp], fy_sem.at[0], fy_sem.at[1], (tm, j)).start())
+        remote(fx_s, fx_r, fx_sem.at[0], fx_sem.at[1], (beside, sp)).start()
+
+    def hand_fields():
         arrived(fy_r.at[pl.ds(0, SPACE - 1)], fy_sem.at[1])
         remote(fy_r, fy, ff_sem.at[0], ff_sem.at[1], (up, sp)).start()
 
@@ -300,9 +311,14 @@
 
             y1[g, pl.ds(sp * R, R)] = s1[g, :, pl.ds(sp * R, R)]
 
+        @pl.when(t == 0)
+        def _():
+            share_fields()
+
         @pl.when(home)
         def _():
             turn_trial()
+            hand_fields()
 
         @pl.when(t == 1 + odd)
         def _():
@@ -417,28 +433,26 @@
     for q in range(1, 4):
         packed = packed + jnp.where(quarter == q, turn(total[8 * q : 8 * q + 8], q * ORB), 0.0)
     p_s[...] = packed
-    p_r[sp] = packed
-    to_peers(lambda j: remote(p_s, p_r.at[sp], p_sem.at[0], p_sem.at[1], (tm, j)).start())
-    arrived(p_r.at[pl.ds(0, SPACE - 1)], p_sem.at[1])
-    q_s[...] = jnp.sum(p_r[...], axis=0) * (1.0 / math.sqrt(C4 * L**3))
 
     @pl.when(even)
     def _():
-        remote(q_s, q_r, q_sem.at[0], q_sem.at[1], (down, sp)).start()
-        arrived(q_r, q_sem.at[1])
+        for j in range(SPACE):
+            remote(p_s, p_r.at[sp], p_sem.at[0], p_sem.at[1], (down, j)).start()
+        arrived(p_r, p_sem.at[1])
 
     @pl.when(odd == 1)
     def _():
-        q_r[...] = q_s[...]
-
-    result = q_r[...]
+        p_r[sp] = packed
+        to_peers(lambda j: remote(p_s, p_r.at[sp], p_sem.at[0], p_sem.at[1], (tm, j)).start())
+        arrived(p_r.at[pl.ds(0, SPACE - 1)], p_sem.at[1])
+
+    result = jnp.sum(p_r[...], axis=0) * (1.0 / math.sqrt(C4 * L**3))
     for q in range(4):
         rows = result if q == 0 else turn(result, K - q * ORB)
         projection[8 * q : 8 * q + 8, :] = rows[:, :ORB]
 
     arrived(fx_s, fx_sem.at[0])
     arrived(fy_s.at[pl.ds(0, SPACE - 1)], fy_sem.at[0])
-    arrived(p_r.at[pl.ds(0, SPACE - 1)], p_sem.at[0])
     for g in range(G):
         arrived(s1.at[g, :, pl.ds(0, L - R)], s1_send.at[g])
         arrived(s2.at[g, :, pl.ds(0, L - R)], s2_send.at[g])
@@ -449,13 +463,28 @@
             arrived(w_in.at[g], z_send.at[g])
         arrived(yh, f_send)
         arrived(fy_r, ff_sem.at[0])
-        arrived(q_s, q_sem.at[0])
+        arrived(p_r, p_sem.at[0])
 
     @pl.when(odd == 1)
     def _():
         arrived(out_v, o_send)
+        arrived(p_r.at[pl.ds(0, SPACE - 1)], p_sem.at[0])
 
     arrived(out_v, o_recv)
+
+
+def leave(handed, projection, handed_out, projection_out, held, in_sems, out_sems):
+    places = [(x, pl.ds(n * (L // 2), L // 2)) for x in range(R) for n in range(2)]
+    reads = [pltpu.make_async_copy(handed.at[p], held.at[p], in_sems.at[n]) for n, p in enumerate(places)]
+    writes = [pltpu.make_async_copy(held.at[p], handed_out.at[p], out_sems.at[n]) for n, p in enumerate(places)]
+    for copy in reads:
+        copy.start()
+    projection_out[...] = projection[...]
+    for read, write in zip(reads, writes):
+        read.wait()
+        write.start()
+    for copy in writes:
+        copy.wait()
 
 
 def body(blocks, fields, trial):
@@ -476,16 +505,14 @@
         pltpu.VMEM((2, R, L, K), bf16), pltpu.VMEM((2, R, L, K), bf16),
         packed, packed, packed,
         pltpu.VMEM((SPACE, R, TRI, 2 * K), f32), pltpu.VMEM((G, R, ROWS, 2 * K), f32),
-        pltpu.VMEM((K, K), f32), tile, pltpu.VMEM((SPACE, 8, K), f32), tile, tile,
+        pltpu.VMEM((K, K), f32), tile, pltpu.VMEM((SPACE, 8, K), f32),
         dma((G,)), dma((G,)), dma(()), dma(()), dma((G,)), dma((G,)), dma((5,)), dma((G,)), dma((5,)), dma(()), dma(()), dma(()),
-        dma((2,)), dma((2,)), dma((2,)), dma((2,)), dma((2,)), dma((9,)),
+        dma((2,)), dma((2,)), dma((2,)), dma((2,)), dma((9,)),
     ]
-    return pl.pallas_call(
+    shapes = (jax.ShapeDtypeStruct(blocks.shape, bf16), jax.ShapeDtypeStruct((ORB, ORB), f32))
+    results = pl.pallas_call(
         lambda *refs: kernel(diagonal, *refs),
-        out_shape=(
-            jax.ShapeDtypeStruct(blocks.shape, bf16),
-            jax.ShapeDtypeStruct((ORB, ORB), f32),
-        ),
+        out_shape=shapes,
         in_specs=[hbm] * (3 + len(mats)),
         out_specs=(hbm, vmem),
         scratch_shapes=scratch,
@@ -493,6 +520,13 @@
             collective_id=0, has_side_effects=True, vmem_limit_bytes=56 * 1024 * 1024
         ),
     )(blocks, fields, trial, *[jnp.asarray(m) for m in mats])
+    return pl.pallas_call(
+        leave,
+        out_shape=shapes,
+        in_specs=[hbm, vmem],
+        out_specs=(hbm, vmem),
+        scratch_shapes=[pltpu.VMEM(blocks.shape, bf16), dma((2 * R,)), dma((2 * R,))],
+    )(*results)
 
 
 def solution(mesh):

time: 74.2 us -> 75 us (1.011)
  Pallas kernels: 69.7 us -> 74.1 us
  local copies, waits for them, and re-layouts: 3.6 us -> 0 us
    pallas_call x1 -> x2, Pallas kernels: 69.7 us -> 74.1 us  [the longest x1 70.5 us: body(): pl.pallas_call(lambda *refs: kernel(diagonal, *refs), out_shape=shapes, i...]
    unnamed x4 -> x0, local copies, waits for them, and re-layouts: 3.6 us -> none
where the time goes in v6:
time: 75 us; the launch traced here: 74.7 us
  Pallas kernels  74.1 us (99%)
    pallas_call x1, Pallas kernels, body(): pl.pallas_call(lambda *refs: kernel(diagonal, *refs), out_shape=shapes, i...  70.5 us
    pallas_call x1, Pallas kernels, body(): pl.pallas_call(leave, out_shape=shapes, in_specs=[hbm, vmem], out_specs=(...  3.59 us

profile of v6, /device:TPU:1, one launch (start us, length us, event | category | flops | bytes accessed | tf_op | source)
XLA Modules:
  0.0 74.7 jit_solution(4732063245244563439)
XLA Ops:
  0.6 70.5 %shard_map.122 = (bf16[3,48,48,128]{3,2,1,0:T(8,128)(2,1)}, f32[32,32]{1,0:T(8,128)}) custom-call(bf16[3,48,48,128]{3,2,1,0:T(8,128)(2,1)} %refs_0_.1, f32[3,48,144]{2,1,0:T(8,128)} %refs_1_.1, bf16[3,48,48,128]{3,2,1,0:T(8,128)(2,1)} %refs_2_.1, bf16[768,768]{1,0:T(8,128)(2,1)} %constant.16.clone.refs_3_, bf16[144,144]{1,0:T(8,128)(2,1)} %constant.17.clone.refs_4_, ...), custom_call_target="tpu_custom_call" | custom-call | tf_op jit(solution)/shard_map/pallas_call | solution.py:513
  71.2 3.6 %shard_map.123 = (bf16[3,48,48,128]{3,2,1,0:T(8,128)(2,1)}, f32[32,32]{1,0:T(8,128)}) custom-call(bf16[3,48,48,128]{3,2,1,0:T(8,128)(2,1)} %get-tuple-element.4.handed, f32[32,32]{1,0:T(8,128)} %get-tuple-element.5.projection), custom_call_target="tpu_custom_call" | custom-call | tf_op jit(solution)/shard_map/pallas_call | solution.py:523

commit v7 on v6

--- a/solution.py
+++ b/solution.py
@@ -94,9 +94,9 @@
     blocks, fields, trial, major_h, minor_h, lanes_h, pack_h, keep_h, spread_h, keep_z_h, fill_h,
     handed, projection,
     fields_v, major, minor, lanes, pack, keep, spread, keep_z, fill,
-    w_in, s1, yh, y1, t1, t2, s2, x2, out_v, trial_v, trial_t, fx_s, fx_r, fy_s, fy_r, fy, c1, c2,
+    w_in, s1, yh, y1, t1, t2, s2, s3, x2, out_v, trial_v, trial_t, fx_s, fx_r, fy_s, fy_r, fy, c1, c2,
     prod, p_s, p_r,
-    z_send, z_recv, h_recv, f_send, f_recv, s1_send, y1_recv, s2_send, x2_recv, o_send, o_recv, tr_sem,
+    z_send, z_recv, h_recv, f_send, f_recv, s1_send, y1_recv, s2_send, x2_recv, m_send, m_recv, o_recv, tr_sem,
     fx_sem, fy_sem, ff_sem, p_sem, in_sem,
 ):
     bf16 = jnp.bfloat16
@@ -106,7 +106,8 @@
     even = odd == 0
     up = lax.rem(tm + 2, TM)
     down = lax.rem(tm + TM - 2, TM)
-    beside = lax.rem(tm + TM - 1 + 2 * odd, TM)
+    after = lax.rem(tm + 1, TM)
+    before = lax.rem(tm + TM - 1, TM)
     my_y = sp // GRID
     my_x = lax.rem(sp, GRID)
     cube = diagonal**3
@@ -145,19 +146,12 @@
     def greet(device):
         pl.semaphore_signal(barrier, inc=1, device_id=device, device_id_type=MESH)
 
-    greet((beside, sp))
+    greet((after, sp))
+    greet((before, sp))
     to_peers(lambda j: greet((tm, j)))
-
-    @pl.when(even)
-    def _():
-        for j in range(SPACE):
-            greet((up, j))
-            greet((down, j))
-
-    @pl.when(odd == 1)
-    def _():
-        greet((up, sp))
-        greet((down, sp))
+    for j in range(SPACE):
+        greet((up, j))
+        greet((down, j))
 
     def own(g):
         for x in range(R):
@@ -170,7 +164,7 @@
 
     own(G - 1)
 
-    pl.semaphore_wait(barrier, SPACE + 2 + 2 * (SPACE - 1) * (1 - odd))
+    pl.semaphore_wait(barrier, 3 * SPACE + 1)
 
     def hand(g):
         for x in range(R):
@@ -201,7 +195,7 @@
         fy_s[...] = dot(pack[...], stacked).astype(bf16).reshape(SPACE, 16, K)
         fy_r[sp] = fy_s[sp]
         to_peers(lambda j: remote(fy_s.at[j], fy_r.at[sp], fy_sem.at[0], fy_sem.at[1], (tm, j)).start())
-        remote(fx_s, fx_r, fx_sem.at[0], fx_sem.at[1], (beside, sp)).start()
+        remote(fx_s, fx_r, fx_sem.at[0], fx_sem.at[1], (after, sp)).start()
 
     def hand_fields():
         arrived(fy_r.at[pl.ds(0, SPACE - 1)], fy_sem.at[1])
@@ -329,6 +323,26 @@
             arrived(yh.at[pl.ds(0, L - R)], h_recv)
             onward(0)
 
+    def back(rows, y):
+        @pl.when(y < R - 1)
+        def _():
+            to_peers(
+                lambda j: remote(
+                    rows.at[y, :, pl.ds(j * R, R)], x2.at[:, :, sp * R + y], s2_send.at[y], x2_recv.at[y], (tm, j)
+                ).start()
+            )
+
+        @pl.when(y == R - 1)
+        def _():
+            for g in range(G):
+                to_peers(
+                    lambda j: remote(
+                        rows.at[y, g, pl.ds(j * R, R)], x2.at[g, :, sp * R + y], s2_send.at[y], x2_recv.at[y + g], (tm, j)
+                    ).start()
+                )
+
+        x2[:, :, sp * R + y] = rows[y, :, pl.ds(sp * R, R)]
+
     @pl.loop(0, R)
     def _(y):
         @pl.when(y == 0)
@@ -372,24 +386,24 @@
         for g in range(G):
             s2[y, g] = moved[:, g * K : (g + 1) * K].reshape(L, ZS, K)
 
-        @pl.when(y < R - 1)
-        def _():
-            to_peers(
-                lambda j: remote(
-                    s2.at[y, :, pl.ds(j * R, R)], x2.at[:, :, sp * R + y], s2_send.at[y], x2_recv.at[y], (tm, j)
-                ).start()
-            )
-
-        @pl.when(y == R - 1)
-        def _():
-            for g in range(G):
-                to_peers(
-                    lambda j: remote(
-                        s2.at[y, g, pl.ds(j * R, R)], x2.at[g, :, sp * R + y], s2_send.at[y], x2_recv.at[y + g], (tm, j)
-                    ).start()
-                )
-
-        x2[:, :, sp * R + y] = s2[y, :, pl.ds(sp * R, R)]
+        @pl.when(even)
+        def _():
+            back(s2, y)
+
+        @pl.when(odd == 1)
+        def _():
+            remote(s2.at[y], s3.at[y], m_send.at[y], m_recv.at[y], (up, sp)).start()
+
+            @pl.when(y > 0)
+            def _():
+                arrived(s3.at[y - 1], m_recv.at[y - 1])
+                back(s3, y - 1)
+
+    @pl.when(odd == 1)
+    def _():
+        turn_trial()
+        arrived(s3.at[R - 1], m_recv.at[R - 1])
+        back(s3, R - 1)
 
     second_coefficients()
     prod[...] = jnp.zeros_like(prod)
@@ -407,23 +421,9 @@
             out_v[g, x] = mixed.reshape(L, ZS, K)
             target = handed.at[x, :, pl.ds(g * ZS, ZS), :]
 
-            @pl.when(even)
-            def _():
-                pltpu.make_async_copy(out_v.at[g, x], target, o_recv).start()
-
-            @pl.when(odd == 1)
-            def _():
-                remote(out_v.at[g, x], target, o_send, o_recv, (up, sp)).start()
-
-        @pl.when(even)
-        def _():
-            products(g)
-
-    @pl.when(odd == 1)
-    def _():
-        turn_trial()
-        for g in range(G):
-            products(g)
+            pltpu.make_async_copy(out_v.at[g, x], target, o_recv).start()
+
+        products(g)
 
     total = prod[:ORB]
     for c in range(1, C4):
@@ -434,24 +434,16 @@
         packed = packed + jnp.where(quarter == q, turn(total[8 * q : 8 * q + 8], q * ORB), 0.0)
     p_s[...] = packed
 
-    @pl.when(even)
-    def _():
-        for j in range(SPACE):
-            remote(p_s, p_r.at[sp], p_sem.at[0], p_sem.at[1], (down, j)).start()
-        arrived(p_r, p_sem.at[1])
-
-    @pl.when(odd == 1)
-    def _():
-        p_r[sp] = packed
-        to_peers(lambda j: remote(p_s, p_r.at[sp], p_sem.at[0], p_sem.at[1], (tm, j)).start())
-        arrived(p_r.at[pl.ds(0, SPACE - 1)], p_sem.at[1])
-
+    for j in range(SPACE):
+        remote(p_s, p_r.at[sp], p_sem.at[0], p_sem.at[1], (down, j)).start()
+    arrived(p_r, p_sem.at[1])
     result = jnp.sum(p_r[...], axis=0) * (1.0 / math.sqrt(C4 * L**3))
     for q in range(4):
         rows = result if q == 0 else turn(result, K - q * ORB)
         projection[8 * q : 8 * q + 8, :] = rows[:, :ORB]
 
     arrived(fx_s, fx_sem.at[0])
+    arrived(p_r, p_sem.at[0])
     arrived(fy_s.at[pl.ds(0, SPACE - 1)], fy_sem.at[0])
     for g in range(G):
         arrived(s1.at[g, :, pl.ds(0, L - R)], s1_send.at[g])
@@ -463,12 +455,11 @@
             arrived(w_in.at[g], z_send.at[g])
         arrived(yh, f_send)
         arrived(fy_r, ff_sem.at[0])
-        arrived(p_r, p_sem.at[0])
 
     @pl.when(odd == 1)
     def _():
-        arrived(out_v, o_send)
-        arrived(p_r.at[pl.ds(0, SPACE - 1)], p_sem.at[0])
+        for y in range(R):
+            arrived(s2.at[y], m_send.at[y])
 
     arrived(out_v, o_recv)
 
@@ -500,13 +491,13 @@
     tile = pltpu.VMEM((8, K), f32)
     scratch = [pltpu.VMEM(fields.shape, f32)] + [pltpu.VMEM(m.shape, m.dtype) for m in mats]
     scratch += [
-        by_x, by_x, pltpu.VMEM((L, R, ZS, K), bf16), by_pair, one_row, one_row, by_x, by_x, by_x, by_x,
+        by_x, by_x, pltpu.VMEM((L, R, ZS, K), bf16), by_pair, one_row, one_row, by_x, by_x, by_x, by_x, by_x,
         pltpu.VMEM((G, K, R * ROWS), bf16),
         pltpu.VMEM((2, R, L, K), bf16), pltpu.VMEM((2, R, L, K), bf16),
         packed, packed, packed,
         pltpu.VMEM((SPACE, R, TRI, 2 * K), f32), pltpu.VMEM((G, R, ROWS, 2 * K), f32),
         pltpu.VMEM((K, K), f32), tile, pltpu.VMEM((SPACE, 8, K), f32),
-        dma((G,)), dma((G,)), dma(()), dma(()), dma((G,)), dma((G,)), dma((5,)), dma((G,)), dma((5,)), dma(()), dma(()), dma(()),
+        dma((G,)), dma((G,)), dma(()), dma(()), dma((G,)), dma((G,)), dma((5,)), dma((G,)), dma((5,)), dma((R,)), dma((R,)), dma(()), dma(()),
         dma((2,)), dma((2,)), dma((2,)), dma((2,)), dma((9,)),
     ]
     shapes = (jax.ShapeDtypeStruct(blocks.shape, bf16), jax.ShapeDtypeStruct((ORB, ORB), f32))

time: 75 us -> 81.5 us (1.087)
  Pallas kernels: 74.1 us -> 80.6 us
    pallas_call x1, Pallas kernels: 70.5 us -> 77 us  [body(): pl.pallas_call(lambda *refs: kernel(diagonal, *refs), out_shape=shapes, i...]
where the time goes in v7:
time: 81.5 us; the launch traced here: 81.2 us
  Pallas kernels  80.6 us (99%)
    pallas_call x1, Pallas kernels, body(): pl.pallas_call(lambda *refs: kernel(diagonal, *refs), out_shape=shapes, i...  77 us
    pallas_call x1, Pallas kernels, body(): pl.pallas_call(leave, out_shape=shapes, in_specs=[hbm, vmem], out_specs=(...  3.59 us

profile of v7, /device:TPU:1, one launch (start us, length us, event | category | flops | bytes accessed | tf_op | source)
XLA Modules:
  0.0 81.2 jit_solution(2892071275476751656)
XLA Ops:
  0.6 77.0 %shard_map.122 = (bf16[3,48,48,128]{3,2,1,0:T(8,128)(2,1)}, f32[32,32]{1,0:T(8,128)}) custom-call(bf16[3,48,48,128]{3,2,1,0:T(8,128)(2,1)} %refs_0_.1, f32[3,48,144]{2,1,0:T(8,128)} %refs_1_.1, bf16[3,48,48,128]{3,2,1,0:T(8,128)(2,1)} %refs_2_.1, bf16[768,768]{1,0:T(8,128)(2,1)} %constant.16.clone.refs_3_, bf16[144,144]{1,0:T(8,128)(2,1)} %constant.17.clone.refs_4_, ...), custom_call_target="tpu_custom_call" | custom-call | tf_op jit(solution)/shard_map/pallas_call | solution.py:504
  77.7 3.6 %shard_map.123 = (bf16[3,48,48,128]{3,2,1,0:T(8,128)(2,1)}, f32[32,32]{1,0:T(8,128)}) custom-call(bf16[3,48,48,128]{3,2,1,0:T(8,128)(2,1)} %get-tuple-element.4.handed, f32[32,32]{1,0:T(8,128)} %get-tuple-element.5.projection), custom_call_target="tpu_custom_call" | custom-call | tf_op jit(solution)/shard_map/pallas_call | solution.py:514

commit v8 on v5

--- a/solution.py
+++ b/solution.py
@@ -95,9 +95,9 @@
     handed, projection,
     fields_v, major, minor, lanes, pack, keep, spread, keep_z, fill,
     w_in, s1, yh, y1, t1, t2, s2, x2, out_v, trial_v, trial_t, fx_s, fx_r, fy_s, fy_r, fy, c1, c2,
-    prod, p_s, p_r, q_s, q_r,
+    prod, p_s, p_r,
     z_send, z_recv, h_recv, f_send, f_recv, s1_send, y1_recv, s2_send, x2_recv, o_send, o_recv, tr_sem,
-    fx_sem, fy_sem, ff_sem, p_sem, q_sem, in_sem,
+    fx_sem, fy_sem, ff_sem, p_sem, in_sem,
 ):
     bf16 = jnp.bfloat16
     tm = lax.axis_index("tm")
@@ -144,9 +144,20 @@
     def greet(device):
         pl.semaphore_signal(barrier, inc=1, device_id=device, device_id_type=MESH)
 
-    for other in (up, down, beside):
-        greet((other, sp))
+    greet((beside, sp))
     to_peers(lambda j: greet((tm, j)))
+
+    @pl.when(even)
+    def _():
+        @pl.loop(0, SPACE)
+        def _(j):
+            greet((up, j))
+            greet((down, j))
+
+    @pl.when(odd == 1)
+    def _():
+        greet((up, sp))
+        greet((down, sp))
 
     def own(g):
         for x in range(R):
@@ -171,7 +182,7 @@
     fy_s[...] = dot(pack[...], stacked).astype(bf16).reshape(SPACE, 16, K)
     fy_r[sp] = fy_s[sp]
 
-    pl.semaphore_wait(barrier, SPACE + 2)
+    pl.semaphore_wait(barrier, SPACE + 2 + 2 * (SPACE - 1) * (1 - odd))
 
     def hand(g):
         for x in range(R):
@@ -417,28 +428,26 @@
     for q in range(1, 4):
         packed = packed + jnp.where(quarter == q, turn(total[8 * q : 8 * q + 8], q * ORB), 0.0)
     p_s[...] = packed
-    p_r[sp] = packed
-    to_peers(lambda j: remote(p_s, p_r.at[sp], p_sem.at[0], p_sem.at[1], (tm, j)).start())
-    arrived(p_r.at[pl.ds(0, SPACE - 1)], p_sem.at[1])
-    q_s[...] = jnp.sum(p_r[...], axis=0) * (1.0 / math.sqrt(C4 * L**3))
 
     @pl.when(even)
     def _():
-        remote(q_s, q_r, q_sem.at[0], q_sem.at[1], (down, sp)).start()
-        arrived(q_r, q_sem.at[1])
+        for j in range(SPACE):
+            remote(p_s, p_r.at[sp], p_sem.at[0], p_sem.at[1], (down, j)).start()
+        arrived(p_r, p_sem.at[1])
 
     @pl.when(odd == 1)
     def _():
-        q_r[...] = q_s[...]
-
-    result = q_r[...]
+        p_r[sp] = packed
+        to_peers(lambda j: remote(p_s, p_r.at[sp], p_sem.at[0], p_sem.at[1], (tm, j)).start())
+        arrived(p_r.at[pl.ds(0, SPACE - 1)], p_sem.at[1])
+
+    result = jnp.sum(p_r[...], axis=0) * (1.0 / math.sqrt(C4 * L**3))
     for q in range(4):
         rows = result if q == 0 else turn(result, K - q * ORB)
         projection[8 * q : 8 * q + 8, :] = rows[:, :ORB]
 
     arrived(fx_s, fx_sem.at[0])
     arrived(fy_s.at[pl.ds(0, SPACE - 1)], fy_sem.at[0])
-    arrived(p_r.at[pl.ds(0, SPACE - 1)], p_sem.at[0])
     for g in range(G):
         arrived(s1.at[g, :, pl.ds(0, L - R)], s1_send.at[g])
         arrived(s2.at[g, :, pl.ds(0, L - R)], s2_send.at[g])
@@ -449,11 +458,12 @@
             arrived(w_in.at[g], z_send.at[g])
         arrived(yh, f_send)
         arrived(fy_r, ff_sem.at[0])
-        arrived(q_s, q_sem.at[0])
+        arrived(p_r, p_sem.at[0])
 
     @pl.when(odd == 1)
     def _():
         arrived(out_v, o_send)
+        arrived(p_r.at[pl.ds(0, SPACE - 1)], p_sem.at[0])
 
     arrived(out_v, o_recv)
 
@@ -476,9 +486,9 @@
         pltpu.VMEM((2, R, L, K), bf16), pltpu.VMEM((2, R, L, K), bf16),
         packed, packed, packed,
         pltpu.VMEM((SPACE, R, TRI, 2 * K), f32), pltpu.VMEM((G, R, ROWS, 2 * K), f32),
-        pltpu.VMEM((K, K), f32), tile, pltpu.VMEM((SPACE, 8, K), f32), tile, tile,
+        pltpu.VMEM((K, K), f32), tile, pltpu.VMEM((SPACE, 8, K), f32),
         dma((G,)), dma((G,)), dma(()), dma(()), dma((G,)), dma((G,)), dma((5,)), dma((G,)), dma((5,)), dma(()), dma(()), dma(()),
-        dma((2,)), dma((2,)), dma((2,)), dma((2,)), dma((2,)), dma((9,)),
+        dma((2,)), dma((2,)), dma((2,)), dma((2,)), dma((9,)),
     ]
     return pl.pallas_call(
         lambda *refs: kernel(diagonal, *refs),

time: 74.2 us -> 73.1 us (0.985)
  Pallas kernels: 69.7 us -> 68.7 us
    pallas_call x1, Pallas kernels: 69.7 us -> 68.7 us  [body(): pl.pallas_call(lambda *refs: kernel(diagonal, *refs), out_shape=(jax.Shap...]
where the time goes in v8:
time: 73.1 us; the launch traced here: 72.9 us
  Pallas kernels  68.7 us (94%)
  local copies, waits for them, and re-layouts  3.6 us (5%)
    pallas_call x1, Pallas kernels, body(): pl.pallas_call(lambda *refs: kernel(diagonal, *refs), out_shape=(jax.Shap...  68.7 us
    unnamed x4, local copies, waits for them, and re-layouts  3.6 us

profile of v8, /device:TPU:1, one launch (start us, length us, event | category | flops | bytes accessed | tf_op | source)
XLA Modules:
  0.0 72.9 jit_solution(841145006165413046)
XLA Ops:
  0.6 68.7 %shard_map.122 = (bf16[3,48,48,128]{3,2,1,0:T(8,128)(2,1)}, f32[32,32]{1,0:T(8,128)}) custom-call(bf16[3,48,48,128]{3,2,1,0:T(8,128)(2,1)} %refs_0_.1, f32[3,48,144]{2,1,0:T(8,128)} %refs_1_.1, bf16[3,48,48,128]{3,2,1,0:T(8,128)(2,1)} %refs_2_.1, bf16[768,768]{1,0:T(8,128)(2,1)} %constant.16.clone.refs_3_, bf16[144,144]{1,0:T(8,128)(2,1)} %constant.17.clone.refs_4_, ...), custom_call_target="tpu_custom_call" | custom-call | tf_op jit(solution)/shard_map/pallas_call | solution.py:493
  69.3 0.0 copy-start
  69.3 3.0 %copy.15 = bf16[3,48,48,128]{3,2,1,0:T(8,128)(2,1)} copy(bf16[3,48,48,128]{3,2,1,0:T(8,128)(2,1)} %get-tuple-element.4) | data formatting | bytes 3538944
  72.3 0.0 copy-done
  72.3 0.6 copy.16
Async XLA Ops:
  69.3 3.0 %copy-start = (f32[32,32]{1,0:T(8,128)S(1)}, f32[32,32]{1,0:T(8,128)}, u32[]{:S(2)}) copy-start(f32[32,32]{1,0:T(8,128)} %get-tuple-element.5) | copy-start | bytes 12292
